TPU v7x, 256 devices: a whole 4x4x8 slice. The times are simulated.
256 devices in a mesh: seq: 32 (over x_lo, z, core), head: 8 (over x_hi, y).
Axes of the slice: x: 4 (x_hi: 2, x_lo: 2; x = x_hi * 2 + x_lo), y: 4, z: 8, core: 2. Of those that a mesh axis runs over, the one named last changes fastest.
Arguments:
- queries: bfloat16 [32768, 4096], P('seq', 'head'), may hold values from -6 to 6
- key_tokens: bfloat16 [32768, 4096], P('seq', 'head'), may hold values from -6 to 6
- value_tokens: bfloat16 [32768, 4096], P('seq', 'head'), may hold values from -6 to 6
- out_weight: bfloat16 [4096, 4096], P('head'), may hold values from -0.09375 to 0.09375
Outputs:
- projected: bfloat16 [32768, 4096], P(('seq', 'head'))
All inputs are finite; a program needn't handle non-finite values.
Results may differ from a plain program's by a relative error of at most 0.015.
Values may be sent and summed in bfloat16 or wider, within the bound.
A program may use at most 128 MiB of HBM per device.

v0:
```python
import math

import jax
import jax.numpy as jnp
from jax import lax
from jax.sharding import PartitionSpec as P

HD = 128
BLK = 256
QG = 16
G1 = 8
WIN = 64
G2 = 32
G3 = 128
G4 = 512


minus_big = -1e30


def passed_along(array, axis, by):
    count = lax.axis_size(axis)
    pairs = [(i, i + by) for i in range(count) if 0 <= i + by < count]
    return lax.ppermute(array, axis, pairs)


def interp_matrix():
    group_count = BLK // QG
    offsets = jnp.arange(BLK, dtype=jnp.int32)
    numer = 2 * offsets - QG + 1
    lower_idx = jnp.clip(numer // (2 * QG), 0, group_count - 2)
    frac = jnp.clip((numer - lower_idx * 2 * QG).astype(jnp.float32) / (2 * QG), 0.0, 1.0)
    columns = jnp.arange(group_count, dtype=jnp.int32)
    left_part = jnp.where(columns[None, :] == lower_idx[:, None], 1.0 - frac[:, None], 0.0)
    right_part = jnp.where(columns[None, :] == lower_idx[:, None] + 1, frac[:, None], 0.0)
    return left_part + right_part


def level_bounds(block_start):
    first = jnp.maximum(block_start - BLK, 0)
    second = jnp.maximum((first - WIN * G1) // G2 * G2, 0)
    third = jnp.maximum((second - WIN * G2) // G3 * G3, 0)
    fourth = jnp.maximum((third - WIN * G3) // G4 * G4, 0)
    lower = jnp.stack([second, third, fourth, jnp.zeros_like(first)], -1)
    upper = jnp.stack([first, second, third, fourth], -1)
    return (lower, upper)


def summary_spans(count, layout):
    per_device = sum((entry[2] for entry in layout))
    row_ids = jnp.arange(count, dtype=jnp.int32)
    device_ids = row_ids // per_device
    local_ids = row_ids % per_device
    low_end = jnp.zeros((count,), jnp.int32)
    span_size = jnp.zeros((count,), jnp.int32)
    level_ids = jnp.full((count,), -1, jnp.int32)
    offset = 0
    for level_id, group_size, per_level in layout:
        inside = (local_ids >= offset) & (local_ids < offset + per_level)
        low_end = jnp.where(
            inside, (device_ids * per_level + local_ids - offset) * group_size, low_end
        )
        span_size = jnp.where(inside, group_size, span_size)
        level_ids = jnp.where(inside, level_id, level_ids)
        offset += per_level
    return (low_end, low_end + span_size, level_ids)


def far_update(carry, pieces, layout, pooled_q, lower, upper):
    run_max, run_den, run_acc = carry
    piece_k, piece_v = pieces
    count = piece_k.shape[0]
    heads_here = pooled_q.shape[2]
    low_end, high_end, level_ids = summary_spans(count, layout)
    pick_low = jnp.zeros((lower.shape[0], count), jnp.int32)
    pick_up = jnp.zeros((lower.shape[0], count), jnp.int32)
    for level_id in range(4):
        match = (level_ids == level_id)[None, :]
        pick_low = jnp.where(match, lower[:, level_id : level_id + 1], pick_low)
        pick_up = jnp.where(match, upper[:, level_id : level_id + 1], pick_up)
    chosen = (low_end[None, :] >= pick_low) & (high_end[None, :] <= pick_up)
    scores = jnp.einsum(
        "bghd,nhd->bhgn",
        pooled_q,
        piece_k.reshape(count, heads_here, HD),
        preferred_element_type=jnp.float32,
    )
    scores = scores * (1.0 / math.sqrt(HD))
    mask = chosen[:, None, None, :]
    new_max = jnp.maximum(run_max, jnp.max(jnp.where(mask, scores, minus_big), axis=-1))
    expo = jnp.where(mask, jnp.exp(scores - new_max[..., None]), 0.0)
    run_den = jnp.sum(expo, axis=-1)
    added = jnp.einsum(
        "bhgn,nhd->bhgd",
        expo.astype(jnp.bfloat16),
        piece_v.reshape(count, heads_here, HD),
        preferred_element_type=jnp.float32,
    )
    run_acc = added
    return (new_max, run_den, run_acc)


def body(queries, key_tokens, value_tokens, out_weight):
    token_count, width = queries.shape
    heads_here = width // HD
    block_count = token_count // BLK
    group_count = BLK // QG
    score_scale = 1.0 / math.sqrt(HD)
    device = lax.axis_index("seq")
    block_starts = device * token_count + jnp.arange(block_count, dtype=jnp.int32) * BLK
    lower, upper = level_bounds(block_starts)
    tails = jnp.stack([key_tokens[token_count - BLK :], value_tokens[token_count - BLK :]])
    before = passed_along(tails, "seq", 1)
    ext_k = jnp.concatenate([before[0], key_tokens]).reshape(block_count + 1, BLK, heads_here, HD)
    ext_v = jnp.concatenate([before[1], value_tokens]).reshape(block_count + 1, BLK, heads_here, HD)
    pair_k = jnp.concatenate([ext_k[:-1], ext_k[1:]], axis=1)
    pair_v = jnp.concatenate([ext_v[:-1], ext_v[1:]], axis=1)
    query_blocks = queries.reshape(block_count, BLK, heads_here, HD)
    scores = (
        jnp.einsum("bqhd,bkhd->bhqk", query_blocks, pair_k, preferred_element_type=jnp.float32)
        * score_scale
    )
    offsets = jnp.arange(BLK, dtype=jnp.int32)[:, None]
    columns = jnp.arange(2 * BLK, dtype=jnp.int32)[None, :]
    valid = (columns <= offsets + BLK)[None] & (
        block_starts[:, None, None] - BLK + columns[None] >= 0
    )
    valid = valid[:, None]
    near_max = jnp.max(jnp.where(valid, scores, minus_big), axis=-1)
    expo = jnp.where(valid, jnp.exp(scores - near_max[..., None]), 0.0)
    near_den = jnp.sum(expo, axis=-1)
    near_num = jnp.einsum(
        "bhqk,bkhd->bhqd", expo.astype(jnp.bfloat16), pair_v, preferred_element_type=jnp.float32
    )
    near_out = near_num / near_den[..., None]
    near_lse = near_max + jnp.log(near_den)
    pooled_q = jnp.mean(
        queries.reshape(block_count, group_count, QG, heads_here, HD), axis=2, dtype=jnp.float32
    ).astype(jnp.bfloat16)
    group_sizes = [G1, G2, G3, G4]
    full_layout = [
        (level_id, size, token_count // size) for level_id, size in enumerate(group_sizes)
    ]

    def pooled_levels(source, layout):
        return jnp.concatenate(
            [
                jnp.mean(
                    source.reshape(token_count // entry[1], entry[1], width),
                    axis=1,
                    dtype=jnp.float32,
                )
                for entry in layout
            ]
        ).astype(jnp.bfloat16)

    init = (
        jnp.full((block_count, heads_here, group_count), minus_big, jnp.float32),
        jnp.zeros((block_count, heads_here, group_count), jnp.float32),
        jnp.zeros((block_count, heads_here, group_count, HD), jnp.float32),
    )
    all_k = pooled_levels(key_tokens, full_layout)
    all_v = pooled_levels(value_tokens, full_layout)
    carry = far_update(
        init,
        (
            lax.all_gather(all_k, "seq", axis=0, tiled=True),
            lax.all_gather(all_v, "seq", axis=0, tiled=True),
        ),
        full_layout,
        pooled_q,
        lower,
        upper,
    )
    run_max, run_den, run_acc = carry
    has_far = block_starts - BLK > 0
    safe_den = jnp.where(has_far[:, None, None], run_den, 1.0)
    far_lse = run_max + jnp.log(safe_den)
    far_out = run_acc / safe_den[..., None]
    weights_interp = interp_matrix()
    tok_lse = jnp.einsum("rg,bhg->bhr", weights_interp, far_lse, precision=lax.Precision.HIGHEST)
    tok_out = jnp.einsum("rg,bhgd->bhrd", weights_interp, far_out, precision=lax.Precision.HIGHEST)
    top_lse = jnp.maximum(near_lse, tok_lse)
    near_weight = jnp.exp(near_lse - top_lse)
    far_weight = jnp.where(has_far[:, None, None], jnp.exp(tok_lse - top_lse), 0.0)
    mixed = (near_weight[..., None] * near_out + far_weight[..., None] * tok_out) / (
        near_weight + far_weight
    )[..., None]
    attention = mixed.transpose(0, 2, 1, 3).reshape(token_count, width).astype(jnp.bfloat16)
    return lax.psum_scatter(
        jnp.dot(attention, out_weight, preferred_element_type=jnp.float32).astype(jnp.bfloat16),
        "head",
        scatter_dimension=0,
        tiled=True,
    )


def solution(mesh):
    in_specs = (P("seq", "head"), P("seq", "head"), P("seq", "head"), P("head", None))
    out_specs = P(("seq", "head"), None)
    return jax.shard_map(body, mesh=mesh, in_specs=in_specs, out_specs=out_specs, check_vma=False)
```

profile of v0, /device:TPU:34, one launch (start us, length us, event | category | flops | bytes accessed | tf_op | source)
XLA Modules:
  0.0 309.0 jit_solution(13720364901968579944)
XLA Ops:
  6.5 1.5 bitcast_reduce_fusion.4
  8.0 1.4 bitcast_reduce_fusion.5
  9.4 1.5 bitcast_reduce_fusion.6
  10.9 2.0 bitcast_reduce_fusion.7
  16.9 2.1 collective-permute-start
  22.3 1.7 reshape.496
  24.1 2.4 copy.34
  26.5 2.4 copy.41
  28.9 2.2 reduce_sum.107
  31.7 1.2 broadcast_and_fusion
  34.3 1.2 copy.40
  36.1 3.1 fusion
  39.2 1.8 fusion.4
  41.0 3.8 %fusion.15 = f32[4,4,256,128]{3,2,1,0:T(8,128)} fusion(f32[4,4,512,256]{3,2,1,0:T(8,128)S(1)} %get-tuple-element.15, f32[4,4,256]{2,1,0:T(4,128)S(1)} %get-tuple-element.14, pred[4,256,512]{1,2,0:T(8,128)(4,1)S(1)} %copy-done.3, bf16[4,256,4,128]{3,1,2,0:T(8,128)(2,1)S(1)} %copy-done.4, bf16[4,256,4,128]{3,1,2,0:T(8,128)(2,1)S(1)} %copy-done.5), kind=kOutput, calls=%fused_computation.20 | convolution fusion | flops 549453824 | bytes 13123584 | tf_op jit(solution)/shard_map/bhqk,bkhd->bhqd/dot_general | solution.py:132
  44.8 40.2 %all-gather.5.cloned.1.call-done = bf16[32,170,512]{2,1,0:T(8,128)(2,1)} async-done(((bf16[1,170,512]{2,1,0:T(8,128)(2,1)}), bf16[32,170,512]{2,1,0:T(8,128)(2,1)}) %all-gather.5.cloned.1.call-update) | async-done | bytes 5570576 | tf_op jit(solution)/shard_map/all_gather | solution.py:167
  85.0 10.6 %reshape.490 = bf16[5440,4,128]{2,1,0:T(4,128)(2,1)} reshape(bf16[32,170,512]{2,1,0:T(8,128)(2,1)} %all-gather.5.cloned.1.call-done) | data formatting | bytes 11141120 | tf_op jit(solution)/shard_map/reshape | solution.py:85
  95.6 4.4 %fusion.11 = f32[4,5440,64]{1,2,0:S(1)} fusion(bf16[4,128,64]{1,2,0:T(8,128)(2,1)S(1)} %bitcast.121, bf16[5440,4,128]{2,1,0:T(4,128)(2,1)} %reshape.490), kind=kOutput, calls=%fused_computation.16 | convolution fusion | flops 356515840 | bytes 11206656
  101.0 3.6 %fusion.14 = (f32[4,4,16]{2,0,1:T(4,128)S(1)}, bf16[4,4,16,5440]{3,2,0,1:T(8,128)(2,1)}) fusion(f32[4,5440,4,16]{1,3,2,0:T(8,128)S(1)} %bitcast.119, f32[4,4,16]{2,0,1:T(4,128)S(1)} %broadcast_maximum_fusion, pred[4,5440]{1,0:T(4,128)(4,1)S(1)} %fusion.47, f32[4,5440,64]{1,2,0:S(1)} %fusion.11), kind=kLoop, calls=%fused_computation.19 | loop fusion | flops 11140864 | bytes 13950208 | tf_op jit(solution)/shard_map/reduce_sum | solution.py:92
  104.7 51.3 %all-gather.7.cloned.1.call-done = bf16[32,170,512]{2,1,0:T(8,128)(2,1)} async-done(((bf16[1,170,512]{2,1,0:T(8,128)(2,1)}), bf16[32,170,512]{2,1,0:T(8,128)(2,1)}) %all-gather.7.cloned.1.call-update) | async-done | bytes 5570576 | tf_op jit(solution)/shard_map/all_gather | solution.py:168
  156.0 10.6 %reshape.491 = bf16[5440,4,128]{2,1,0:T(4,128)(2,1)} reshape(bf16[32,170,512]{2,1,0:T(8,128)(2,1)} %all-gather.7.cloned.1.call-done) | data formatting | bytes 11141120 | tf_op jit(solution)/shard_map/reshape | solution.py:96
  166.6 4.7 %fusion.38 = f32[4,4,16,128]{3,2,1,0:T(8,128)S(1)} fusion(bf16[4,4,16,5440]{3,2,0,1:T(8,128)(2,1)} %get-tuple-element.13, bf16[5440,4,128]{2,1,0:T(4,128)(2,1)} %reshape.491, f32[4,4,16]{2,1,0:T(4,128)S(1)} %copy.45), kind=kOutput, calls=%fused_computation.48 | convolution fusion | flops 356548608 | bytes 8487936 | tf_op jit(solution)/shard_map/bhgn,nhd->bhgd/dot_general | solution.py:93
  171.5 3.7 %fusion.31 = bf16[4,256,4,128]{3,1,2,0:T(8,128)(2,1)S(1)} fusion(f32[4,4,256,128]{3,2,1,0:T(8,128)S(1)} %copy-done.7, f32[4,4,16,128]{3,2,1,0:T(8,128)S(1)} %fusion.38, f32[4,256,4]{1,2,0:T(4,128)S(1)} %get-tuple-element.5, f32[4,256,4]{1,2,0:T(4,128)S(1)} %get-tuple-element.6, f32[4,256,4]{1,2,0:T(4,128)S(1)} %bitcast.122, ...), kind=kOutput, calls=%fused_computation.36 | convolution fusion | flops 103829504 | bytes 3346432 | tf_op jit(solution)/shard_map/rg,bhgd->bhrd/dot_general | solution.py:182
  176.0 6.7 %convolution_convert_fusion = bf16[1024,4096]{1,0:T(8,128)(2,1)} fusion(bf16[512,4096]{1,0:T(8,128)(2,1)S(1)} %copy-done.6, bf16[128,8,4,128]{3,2,1,0:T(4,128)(2,1)S(1)} %bitcast.120), kind=kOutput, calls=%fused_computation.5 | convolution fusion | flops 4299161600 | bytes 13631488 | tf_op jit(solution)/shard_map/dot_general | solution.py:191
  182.7 119.8 %reduce-scatter.2.cloned.1.call-done = bf16[128,4096]{1,0:T(8,128)(2,1)} async-done(((bf16[1024,4096]{1,0:T(8,128)(2,1)}), bf16[128,4096]{1,0:T(8,128)(2,1)}) %reduce-scatter.2.cloned.1.call-update) | async-done | bytes 1048592 | tf_op jit(solution)/shard_map/reduce_scatter | solution.py:190
  (70 shorter events, 11.8 us)
Async XLA Ops:
  6.5 7.3 %copy-start = (bf16[1024,512]{1,0:T(8,128)(2,1)S(1)}, bf16[1024,512]{1,0:T(8,128)(2,1)}, u32[]{:S(2)}) copy-start(bf16[1024,512]{1,0:T(8,128)(2,1)} %param.6) | copy-start | bytes 3145732
  6.5 78.4 %all-gather.5.cloned.1.call-start = ((), (), s32[]{:S(2)}) async-start(), calls=%async_computation.2 | async-start | bytes 5947392 | tf_op jit(solution)/shard_map/all_gather | solution.py:167
  10.9 5.1 %copy-start.1 = (bf16[1024,512]{1,0:T(8,128)(2,1)S(1)}, bf16[1024,512]{1,0:T(8,128)(2,1)}, u32[]{:S(2)}) copy-start(bf16[1024,512]{1,0:T(8,128)(2,1)} %param.5) | copy-start | bytes 3145732
  13.7 142.3 %all-gather.7.cloned.1.call-start = ((), (), s32[]{:S(2)}) async-start(), calls=%async_computation.3 | async-start | bytes 5947392 | tf_op jit(solution)/shard_map/all_gather | solution.py:168
  14.4 6.8 %copy-start.2 = (bf16[1024,512]{1,0:T(8,128)(2,1)S(1)}, bf16[1024,512]{1,0:T(8,128)(2,1)}, u32[]{:S(2)}) copy-start(bf16[1024,512]{1,0:T(8,128)(2,1)} %param.4) | copy-start | bytes 3145732
  15.9 286.6 %reduce-scatter.2.cloned.1.call-start = ((), (), s32[]{:S(2)}) async-start(), calls=%async_computation.1 | async-start | bytes 9437184 | tf_op jit(solution)/shard_map/reduce_scatter | solution.py:190
  16.9 16.0 %collective-permute-start = (bf16[2,256,512]{2,1,0:T(8,128)(2,1)}, bf16[2,256,512]{2,1,0:T(8,128)(2,1)}, u32[]{:S(2)}, u32[]{:S(2)}) collective-permute-start(bf16[2,256,512]{2,1,0:T(8,128)(2,1)} %pad_maximum_fusion.2), channel_id=1, source_target_pairs={{0,8},{8,16},{16,24},{24,32},{32,40},{40,48},{48,56},{56,64},{64,7... | collective-permute-start | bytes 1572872 | tf_op jit(solution)/shard_map/ppermute | solution.py:24
  34.3 1.7 copy-start.3
  39.1 1.9 copy-start.4
  39.2 1.9 copy-start.5
  166.6 4.9 %copy-start.7 = (f32[4,4,256,128]{3,2,1,0:T(8,128)S(1)}, f32[4,4,256,128]{3,2,1,0:T(8,128)}, u32[]{:S(2)}) copy-start(f32[4,4,256,128]{3,2,1,0:T(8,128)} %fusion.15) | copy-start | bytes 6291460
  171.5 4.5 %copy-start.6 = (bf16[512,4096]{1,0:T(8,128)(2,1)S(1)}, bf16[512,4096]{1,0:T(8,128)(2,1)}, u32[]{:S(2)}) copy-start(bf16[512,4096]{1,0:T(8,128)(2,1)} %param.7) | copy-start | bytes 12582916
Sparse Core Ops, SparseCore 0:
  13.9 71.0 all-gather.4
  86.8 69.1 all-gather.6
  182.8 119.6 reduce-scatter.1
where the time goes:
time: 311 us; the launch traced here: 309 us
  waiting for transfers between devices  211 us (68%)
  local copies, waits for them, and re-layouts  35 us (11%)
  matrix products  26.4 us (8%)
  other arithmetic  20.6 us (7%)
  between operations  13.5 us (4%)
    reduce_scatter x1, waiting for transfers between devices, body(): lax.psum_scatter(jnp.dot(attention, out_weight, preferred_element_type=jn...  120 us
    all_gather x1, waiting for transfers between devices, body(): lax.all_gather(all_v, 'seq', axis=0, tiled=True)  51.3 us
    all_gather x1, waiting for transfers between devices, body(): lax.all_gather(all_k, 'seq', axis=0, tiled=True)  40.2 us
    reshape x1, local copies, waits for them, and re-layouts, far_update(): piece_v.reshape(count, heads_here, HD)  10.6 us
    reshape x1, local copies, waits for them, and re-layouts, far_update(): piece_k.reshape(count, heads_here, HD)  10.6 us
    reduce_sum x8, other arithmetic, pooled_levels(): jnp.mean(source.reshape(token_count // entry[1], entry[1], width), axis=1...  7.71 us
    dot_general x1, matrix products, body(): jnp.dot(attention, out_weight, preferred_element_type=jnp.float32)  6.69 us
  transfers between devices with their start and end apart: 4, of which 3 were waited for; matrix products, arithmetic and copies ran while one was open for 16% of the time, Pallas kernels for 0%

commit v1 on v0

v1 whole, which is shorter than its diff:
```python
import functools
import math

import jax
import jax.numpy as jnp
from jax import lax
from jax.experimental import pallas as pl
from jax.experimental.pallas import tpu as pltpu
from jax.sharding import PartitionSpec as P

MESH = pl.DeviceIdType.MESH
HD = 128
BLK = 256
QG = 16
LOG2E = 1.4426950408889634
SCALE2 = LOG2E / math.sqrt(HD)
BIG = -1e30
F32 = jnp.float32
BF16 = jnp.bfloat16

NEAR3 = 3
LAST3 = 11
ROW4 = 288


def iota(shape, dim):
    return lax.broadcasted_iota(jnp.int32, shape, dim)


def dot_nt(a, b):
    return lax.dot_general(a, b, (((1,), (1,)), ((), ())), preferred_element_type=F32)


def dot_nn(a, b):
    return jnp.dot(a, b, preferred_element_type=F32)


def fill_pool_matrix(pm):
    def piece(rows, shift, weight):
        hit = (iota((rows, 1024), 1) >> shift) == iota((rows, 1024), 0)
        return jnp.where(hit, weight, 0.0).astype(BF16)

    pm[0:128, :] = piece(128, 3, 1.0 / 8)
    pm[128:160, :] = piece(32, 5, 1.0 / 32)
    row, col = iota((16, 1024), 0), iota((16, 1024), 1)
    third = jnp.where((col >> 7) == row, 1.0 / 128, 0.0)
    fourth = jnp.where((col >> 9) == (row & 1), 1.0 / 512, 0.0)
    pm[160:176, :] = jnp.where(row < 8, third, fourth).astype(BF16)
    pm[176:240, :] = piece(64, 4, 1.0 / 16)


def fill_interp(wi):
    row, col = iota((BLK, 48), 0), iota((BLK, 48), 1)
    numer = 2 * row - (QG - 1)
    low = jnp.clip(numer >> 5, 0, BLK // QG - 2)
    frac = jnp.clip((numer - low * 32).astype(F32) * (1.0 / 32), 0.0, 1.0)
    group = col & 15
    value = jnp.where(group == low, 1.0 - frac, 0.0) + jnp.where(group == low + 1, frac, 0.0)
    wi[...] = value.astype(BF16)


def bounds(start):
    first = jnp.maximum(start - 256, 0)
    second = jnp.maximum(((first - 512) >> 5) << 5, 0)
    third = jnp.maximum(((second - 2048) >> 7) << 7, 0)
    fourth = jnp.maximum(((third - 8192) >> 9) << 9, 0)
    return first, second, third, fourth


def fill_masks(pick12, pick34, s0):
    shape = (64, 256)
    first, second, third, fourth = bounds(s0 + 256 * (iota(shape, 0) >> 4))
    col = iota(shape, 1)
    is_first = col < 160
    token = jnp.where(is_first, s0 - 768 + 8 * col, s0 - 3072 + 32 * (col - 160))
    size = jnp.where(is_first, 8, 32)
    lower = jnp.where(is_first, second, third)
    upper = jnp.where(is_first, first, second)
    pick12[...] = jnp.where((token >= lower) & (token + size <= upper), 1, 0)
    shape = (64, 640)
    first, second, third, fourth = bounds(s0 + 256 * (iota(shape, 0) >> 4))
    col = iota(shape, 1)
    is_third = col < ROW4
    rest = col - ROW4
    token3 = s0 - LAST3 * 1024 + (col >> 5) * 1024 + (col & 7) * 128
    token4 = s0 - (LAST3 + (rest >> 4)) * 1024 + (rest & 1) * 512
    token = jnp.where(is_third, token3, token4)
    size = jnp.where(is_third, 128, 512)
    head = jnp.where(is_third, (col & 31) >> 3, (rest & 15) >> 1)
    lower = jnp.where(is_third, fourth, 0)
    upper = jnp.where(is_third, third, fourth)
    chosen = (token >= lower) & (token + size <= upper)
    pick34[...] = jnp.where(chosen, head, -1)


def kernel(
    n, q_hbm, k_hbm, v_hbm, att,
    kvx, qs, pm, wi, res, pool12, own34, qp, far12, far34, pick12, pick34, fo, num, mx, den,
    load_sem, send_sem, recv_sem,
):
    me = lax.axis_index("seq")
    s0 = me * 1024

    loads = [
        pltpu.make_async_copy(k_hbm, kvx.at[256:1280, 0:512], load_sem.at[0]),
        pltpu.make_async_copy(v_hbm, kvx.at[256:1280, 512:1024], load_sem.at[1]),
        pltpu.make_async_copy(q_hbm, qs, load_sem.at[2]),
    ]
    for load in loads:
        load.start()

    kvx[0:256, :] = jnp.zeros((256, 1024), BF16)
    far12[...] = jnp.zeros(far12.shape, BF16)
    far34[...] = jnp.zeros(far34.shape, BF16)

    barrier = pltpu.get_barrier_semaphore()

    def greet(k, carry):
        @pl.when(me - k >= 0)
        def _():
            pl.semaphore_signal(barrier, inc=1, device_id={"seq": me - k}, device_id_type=MESH)
        return carry

    lax.fori_loop(1, n, greet, 0)

    fill_pool_matrix(pm)
    for load in loads:
        load.wait()

    def pool(c, carry):
        cols = pl.ds(pl.multiple_of(c * 256, 256), 256)
        res[:, cols] = dot_nn(pm[0:176, :], kvx[256:1280, cols])
        return carry

    lax.fori_loop(0, 4, pool, 0)
    pool12[...] = res[0:160, :].astype(BF16)
    row8 = iota((8, 128), 0)
    sides = []
    for side in range(2):
        tiles = [res[160:168, side * 512 + h * 128 : side * 512 + (h + 1) * 128] for h in range(4)]
        last = jnp.zeros((8, 128), F32)
        for h in range(4):
            lanes = slice(side * 512 + h * 128, side * 512 + (h + 1) * 128)
            last = jnp.where((row8 >> 1) == h, res[168:176, lanes], last)
        sides.append(jnp.concatenate(tiles + [last, jnp.zeros((8, 128), F32)], axis=0))
    own34[...] = jnp.concatenate(sides, axis=1).astype(BF16)
    far12[96:160, :] = pool12[0:64, :]

    @pl.when(me < n - 1)
    def _():
        pl.semaphore_wait(barrier, n - 1 - me)

    def to_later(k, src, dst, slot):
        return pltpu.make_async_remote_copy(
            src_ref=src, dst_ref=dst, send_sem=send_sem.at[slot], recv_sem=recv_sem.at[slot],
            device_id={"seq": lax.rem(me + k, n)}, device_id_type=MESH,
        )

    def copy_tail():
        return to_later(1, kvx.at[1024:1280], kvx.at[0:256], 0)

    def copy1():
        return to_later(1, pool12.at[32:128], far12.at[0:96], 1)

    def copy2(k):
        row = 160 + 32 * (3 - k)
        return to_later(k, pool12.at[128:160], far12.at[row : row + 32], 1 + k)

    def copy3(k):
        row = pl.multiple_of((LAST3 - k) * 32, 32)
        return to_later(k, own34.at[0:32], far34.at[pl.ds(row, 32)], 5 + k - NEAR3)

    def copy4(k):
        row = pl.multiple_of(ROW4 + (k - LAST3) * 16, 16)
        return to_later(k, own34.at[32:48], far34.at[pl.ds(row, 16)], 14 + k - LAST3)

    def each(apply, condition):
        @pl.when(condition(1))
        def _():
            apply(copy1())
        for k in (1, 2, 3):
            @pl.when(condition(k))
            def _():
                apply(copy2(k))

        def third(k, carry):
            @pl.when(condition(k))
            def _():
                apply(copy3(k))
            return carry

        def fourth(k, carry):
            @pl.when(condition(k))
            def _():
                apply(copy4(k))
            return carry

        lax.fori_loop(NEAR3, LAST3 + 1, third, 0)
        lax.fori_loop(LAST3, n, fourth, 0)

    has_later = lambda k: me + k < n
    has_earlier = lambda k: me - k >= 0

    @pl.when(has_later(1))
    def _():
        copy_tail().start()

    each(lambda copy: copy.start(), has_later)

    qp[...] = dot_nn(pm[176:240, :], qs[...]).astype(BF16)
    fill_interp(wi)
    fill_masks(pick12, pick34, s0)

    def near(b, h):
        rows = pl.ds(pl.multiple_of(b * 256, 256), 256)
        next_rows = pl.ds(pl.multiple_of(b * 256 + 256, 256), 256)
        lanes = pl.ds(pl.multiple_of(h * 128, 128), 128)
        vlanes = pl.ds(pl.multiple_of(512 + h * 128, 128), 128)
        q = qs[rows, lanes]
        s_prev = dot_nt(q, kvx[rows, lanes])
        s_own = dot_nt(q, kvx[next_rows, lanes])
        s_prev = jnp.where(s0 + b * 256 > 0, s_prev, BIG)
        s_own = jnp.where(iota((256, 256), 1) <= iota((256, 256), 0), s_own, BIG)
        top = jnp.max(jnp.maximum(s_prev, s_own), axis=1, keepdims=True) * SCALE2
        w_prev = jnp.exp2(s_prev * SCALE2 - top)
        w_own = jnp.exp2(s_own * SCALE2 - top)
        total = jnp.sum(w_prev + w_own, axis=1, keepdims=True)
        num[rows, lanes] = dot_nn(w_prev.astype(BF16), kvx[rows, vlanes]) + dot_nn(
            w_own.astype(BF16), kvx[next_rows, vlanes]
        )
        mx[rows, lanes] = jnp.broadcast_to(top, (256, 128))
        den[rows, lanes] = jnp.broadcast_to(total, (256, 128))

    def near_step(i, carry):
        near(i >> 2, i & 3)
        return carry

    lax.fori_loop(4, 16, near_step, 0)

    @pl.when(has_earlier(1))
    def _():
        copy_tail().wait_recv()

    lax.fori_loop(0, 4, near_step, 0)

    each(lambda copy: copy.wait_recv(), has_earlier)

    def far(h, carry):
        lanes = pl.ds(pl.multiple_of(h * 128, 128), 128)
        vlanes = pl.ds(pl.multiple_of(512 + h * 128, 128), 128)
        pooled = qp[:, lanes]
        in12 = pick12[...] > 0
        in34 = pick34[...] == h
        s12 = jnp.where(in12, dot_nt(pooled, far12[:, lanes]), BIG)
        s34 = jnp.where(in34, dot_nt(pooled, far34[:, 0:128]), BIG)
        top = jnp.maximum(jnp.max(s12, axis=1, keepdims=True), jnp.max(s34, axis=1, keepdims=True)) * SCALE2
        w12 = jnp.where(in12, jnp.exp2(s12 * SCALE2 - top), 0.0)
        w34 = jnp.where(in34, jnp.exp2(s34 * SCALE2 - top), 0.0)
        total = jnp.sum(w12, axis=1, keepdims=True) + jnp.sum(w34, axis=1, keepdims=True)
        acc = dot_nn(w12.astype(BF16), far12[:, vlanes]) + dot_nn(w34.astype(BF16), far34[:, 128:256])
        some = total > 0
        safe = jnp.where(some, total, 1.0)
        lse = jnp.where(some, top + jnp.log(safe) * LOG2E, BIG)
        both = jnp.concatenate([acc / safe, jnp.broadcast_to(lse, (64, 128))], axis=1)
        high = both.astype(BF16)
        rest = both - high.astype(F32)
        middle = rest.astype(BF16)
        low = (rest - middle.astype(F32)).astype(BF16)
        for b in range(4):
            for j, part in enumerate((high, middle, low)):
                fo[h * 4 + b, 16 * j : 16 * (j + 1), :] = part[16 * b : 16 * (b + 1), :]
        return carry

    lax.fori_loop(0, 4, far, 0)

    def mix(i, carry):
        b, h = i >> 2, i & 3
        rows = pl.ds(pl.multiple_of(b * 256, 256), 256)
        lanes = pl.ds(pl.multiple_of(h * 128, 128), 128)
        tok = dot_nn(wi[...], fo[h * 4 + b])
        tok_out, tok_lse = tok[:, 0:128], tok[:, 128:256]
        near_max = mx[rows, lanes]
        top = jnp.maximum(near_max, tok_lse)
        a = jnp.exp2(near_max - top)
        b_far = jnp.exp2(tok_lse - top)
        mixed = (num[rows, lanes] * a + tok_out * b_far) / (den[rows, lanes] * a + b_far)
        att[rows, lanes] = mixed.astype(BF16)
        return carry

    lax.fori_loop(0, 16, mix, 0)

    @pl.when(has_later(1))
    def _():
        copy_tail().wait_send()

    each(lambda copy: copy.wait_send(), has_later)


def attention(n, q, k, v):
    any_spec = pl.BlockSpec(memory_space=pl.ANY)
    vm = pltpu.VMEM
    return pl.pallas_call(
        functools.partial(kernel, n),
        out_shape=jax.ShapeDtypeStruct(q.shape, BF16),
        in_specs=[any_spec] * 3,
        out_specs=pl.BlockSpec(memory_space=pltpu.VMEM),
        scratch_shapes=[
            vm((1280, 1024), BF16),
            vm((1024, 512), BF16),
            vm((240, 1024), BF16),
            vm((256, 48), BF16),
            vm((176, 1024), F32),
            vm((160, 1024), BF16),
            vm((48, 256), BF16),
            vm((64, 512), BF16),
            vm((256, 1024), BF16),
            vm((640, 256), BF16),
            vm((64, 256), jnp.int32),
            vm((64, 640), jnp.int32),
            vm((16, 48, 256), BF16),
            vm((1024, 512), F32),
            vm((1024, 512), F32),
            vm((1024, 512), F32),
            pltpu.SemaphoreType.DMA((3,)),
            pltpu.SemaphoreType.DMA((35,)),
            pltpu.SemaphoreType.DMA((35,)),
        ],
        compiler_params=pltpu.CompilerParams(
            collective_id=0, has_side_effects=True, vmem_limit_bytes=48 * 1024 * 1024
        ),
        cost_estimate=pl.CostEstimate(flops=2 * 10**9, bytes_accessed=4 * 2**20, transcendentals=2 * 10**6),
    )(q, k, v)


def solution(mesh):
    n = mesh.shape["seq"]

    def body(queries, key_tokens, value_tokens, out_weight):
        att = attention(n, queries, key_tokens, value_tokens)
        share = jnp.dot(att, out_weight, preferred_element_type=F32).astype(BF16)
        return lax.psum_scatter(share, "head", scatter_dimension=0, tiled=True)

    in_specs = (P("seq", "head"), P("seq", "head"), P("seq", "head"), P("head", None))
    out_specs = P(("seq", "head"), None)
    return jax.shard_map(body, mesh=mesh, in_specs=in_specs, out_specs=out_specs, check_vma=False)
```

time: 311 us -> 181 us (0.58)
  waiting for transfers between devices: 211 us -> 121 us
  Pallas kernels: 0 us -> 33.8 us
  local copies, waits for them, and re-layouts: 35 us -> 3.68 us
  other arithmetic: 20.6 us -> 0 us
  matrix products: 26.4 us -> 6.79 us
    all_gather x2 -> x0, waiting for transfers between devices: 91.5 us -> none  [the longest x1 51.3 us: body(): lax.all_gather(all_v, 'seq', axis=0, tiled=True)]
    pallas_call x0 -> x1, Pallas kernels: none -> 33.8 us  [attention(): pl.pallas_call(functools.partial(kernel, n), out_shape=jax.ShapeDtypeStru...]
    reshape x3 -> x0, local copies, waits for them, and re-layouts: 22.2 us -> none  [the longest x1 10.6 us: far_update(): piece_v.reshape(count, heads_here, HD)]
    reduce_sum x11 -> x0, other arithmetic: 15.4 us -> none  [the longest x8 7.71 us: pooled_levels(): jnp.mean(source.reshape(token_count // entry[1], entry[1], width), axis=1...]
    dot_general x6 -> x1, matrix products: 22 us -> 6.79 us  [body(): share = jnp.dot(att, out_weight, preferred_element_type=F32).astype(BF16)]
    slice x8 -> x0, local copies, waits for them, and re-layouts: 9 us -> none  [the longest x4 4.98 us: body(): pair_v = jnp.concatenate([ext_v[:-1], ext_v[1:]], axis=1)]
    unnamed x1 -> x0, matrix products: 4.41 us -> none
    unnamed x16 -> x8, local copies, waits for them, and re-layouts: 0.04 us -> 3.68 us
  transfers between devices with their start and end apart: 4 -> 1, of which waited for: 3 -> 1; matrix products, arithmetic and copies ran while one was open for 16% -> 0% of each run, Pallas kernels for 0% -> 0%
where the time goes in v1:
time: 181 us; the launch traced here: 179 us
  waiting for transfers between devices  121 us (67%)
  Pallas kernels  33.8 us (19%)
  between operations  13.4 us (7%)
  matrix products  6.79 us (4%)
  local copies, waits for them, and re-layouts  3.68 us (2%)
    reduce_scatter x1, waiting for transfers between devices, body(): return lax.psum_scatter(share, 'head', scatter_dimension=0, tiled=True)  121 us
    pallas_call x1, Pallas kernels, attention(): pl.pallas_call(functools.partial(kernel, n), out_shape=jax.ShapeDtypeStru...  33.8 us
    dot_general x1, matrix products, body(): share = jnp.dot(att, out_weight, preferred_element_type=F32).astype(BF16)  6.79 us
    unnamed x8, local copies, waits for them, and re-layouts  3.68 us
  transfers between devices with their start and end apart: 1, of which 1 were waited for; matrix products, arithmetic and copies ran while one was open for 0% of the time, Pallas kernels for 0%

profile of v1, /device:TPU:34, one launch (start us, length us, event | category | flops | bytes accessed | tf_op | source)
XLA Modules:
  0.0 178.9 jit_solution(2183620016843478805)
XLA Ops:
  6.5 0.0 reduce-scatter.2.cloned.1.call-start
  6.5 0.0 copy-start
  6.5 1.2 copy-done
  7.8 0.0 copy-start.1
  7.8 1.2 copy-done.1
  9.0 0.0 copy-start.2
  9.0 1.2 copy-done.2
  10.2 0.0 copy-start.3
  10.2 33.8 %shard_map.46 = bf16[1024,512]{1,0:T(8,128)(2,1)S(1)} custom-call(bf16[1024,512]{1,0:T(8,128)(2,1)S(1)} %copy-done, bf16[1024,512]{1,0:T(8,128)(2,1)S(1)} %copy-done.1, bf16[1024,512]{1,0:T(8,128)(2,1)S(1)} %copy-done.2), custom_call_target="tpu_custom_call" | custom-call | flops 2000000000 | bytes 4194304 | tf_op jit(solution)/shard_map/pallas_call | solution.py:302
  44.0 0.0 copy-done.3
  44.1 6.8 %convolution_convert_fusion = bf16[1024,4096]{1,0:T(8,128)(2,1)} fusion(bf16[1024,512]{1,0:T(8,128)(2,1)S(1)} %shard_map.46, bf16[512,4096]{1,0:T(8,128)(2,1)S(1)} %copy-done.3), kind=kOutput, calls=%fused_computation | convolution fusion | flops 4299161600 | bytes 13631488 | tf_op jit(solution)/shard_map/dot_general | solution.py:340
  50.8 0.0 reduce-scatter.2.cloned.1.call-update
  50.9 121.2 %reduce-scatter.2.cloned.1.call-done = bf16[128,4096]{1,0:T(8,128)(2,1)} async-done(((bf16[1024,4096]{1,0:T(8,128)(2,1)}), bf16[128,4096]{1,0:T(8,128)(2,1)}) %reduce-scatter.2.cloned.1.call-update) | async-done | bytes 1048592 | tf_op jit(solution)/shard_map/reduce_scatter | solution.py:341
Async XLA Ops:
  6.5 165.5 %reduce-scatter.2.cloned.1.call-start = ((), (), s32[]{:S(2)}) async-start(), calls=%async_computation.1 | async-start | bytes 9437184 | tf_op jit(solution)/shard_map/reduce_scatter | solution.py:341
  6.5 1.2 copy-start
  7.8 1.2 copy-start.1
  9.0 1.2 copy-start.2
  10.2 33.8 %copy-start.3 = (bf16[512,4096]{1,0:T(8,128)(2,1)S(1)}, bf16[512,4096]{1,0:T(8,128)(2,1)}, u32[]{:S(2)}) copy-start(bf16[512,4096]{1,0:T(8,128)(2,1)} %param.7) | copy-start | bytes 12582916
Sparse Core Ops, SparseCore 0:
  51.0 121.0 reduce-scatter.1

commit v2 on v1

--- a/solution.py
+++ b/solution.py
@@ -94,18 +94,30 @@
 
 
 def kernel(
-    n, q_hbm, k_hbm, v_hbm, att,
+    n, q_hbm, k_hbm, v_hbm, w_hbm, out,
     kvx, qs, pm, wi, res, pool12, own34, qp, far12, far34, pick12, pick34, fo, num, mx, den,
-    load_sem, send_sem, recv_sem,
+    att, att_in, w_own, w_in, sb1, rb1, sb2, rb2, own,
+    load_sem, send_sem, recv_sem, att_send, att_recv, w_send, w_recv, send1, recv1, send2, recv2,
 ):
     me = lax.axis_index("seq")
+    head = lax.axis_index("head")
     s0 = me * 1024
+    half = lax.div(head, 4)
+    y = lax.rem(head, 4)
+    partner = lax.rem(head + 4, 8)
+    up = half * 4 + lax.rem(y + 1, 4)
+    down = half * 4 + lax.rem(y + 3, 4)
+    across = {"seq": lax.rem(me + n // 2, n), "head": partner}
+    quarter = lax.rem(me, 4)
+    sibling = me + 1 - 2 * lax.rem(me, 2)
+    beside = me + 2 - 4 * lax.div(quarter, 2)
 
     loads = [
         pltpu.make_async_copy(k_hbm, kvx.at[256:1280, 0:512], load_sem.at[0]),
         pltpu.make_async_copy(v_hbm, kvx.at[256:1280, 512:1024], load_sem.at[1]),
         pltpu.make_async_copy(q_hbm, qs, load_sem.at[2]),
     ]
+    load_w = pltpu.make_async_copy(w_hbm, w_own, load_sem.at[3])
     for load in loads:
         load.start()
 
@@ -122,6 +134,8 @@
         return carry
 
     lax.fori_loop(1, n, greet, 0)
+    for place in ({"head": partner}, {"head": up}, {"head": down}, across, {"seq": sibling}, {"seq": beside}):
+        pl.semaphore_signal(barrier, inc=1, device_id=place, device_id_type=MESH)
 
     fill_pool_matrix(pm)
     for load in loads:
@@ -146,9 +160,8 @@
     own34[...] = jnp.concatenate(sides, axis=1).astype(BF16)
     far12[96:160, :] = pool12[0:64, :]
 
-    @pl.when(me < n - 1)
-    def _():
-        pl.semaphore_wait(barrier, n - 1 - me)
+    pl.semaphore_wait(barrier, n - 1 - me + 6)
+    load_w.start()
 
     def to_later(k, src, dst, slot):
         return pltpu.make_async_remote_copy(
@@ -206,6 +219,33 @@
         copy_tail().start()
 
     each(lambda copy: copy.start(), has_later)
+
+    def w_copy(src, kind, j, rows_of, place):
+        rows = pl.ds(pl.multiple_of(rows_of * 128, 128), 128)
+        cols = pl.ds(pl.multiple_of(j * 1024, 1024), 1024)
+        return pltpu.make_async_remote_copy(
+            src_ref=src.at[rows, cols], dst_ref=w_in.at[rows, cols],
+            send_sem=w_send.at[kind * 4 + j], recv_sem=w_recv.at[kind * 4 + j],
+            device_id=place, device_id_type=MESH,
+        )
+
+    other = lax.rem(quarter + 2, 4)
+    w_across = lambda j: w_copy(w_hbm, 0, j, quarter, across)
+    w_sibling = lambda j: w_copy(w_in, 1, j, quarter, {"seq": sibling})
+    w_beside = lambda j: w_copy(w_in, 2, j, quarter, {"seq": beside})
+    w_last = lambda j: w_copy(w_in, 3, j, other, {"seq": sibling})
+
+    def pass_on(j):
+        w_across(j).wait_recv()
+        w_sibling(j).start()
+        w_beside(j).start()
+
+    def pass_last(j):
+        w_beside(j).wait_recv()
+        w_last(j).start()
+
+    for j in range(4):
+        w_across(j).start()
 
     qp[...] = dot_nn(pm[176:240, :], qs[...]).astype(BF16)
     fill_interp(wi)
@@ -236,6 +276,7 @@
         return carry
 
     lax.fori_loop(4, 16, near_step, 0)
+    pass_on(0)
 
     @pl.when(has_earlier(1))
     def _():
@@ -273,36 +314,137 @@
 
     lax.fori_loop(0, 4, far, 0)
 
-    def mix(i, carry):
-        b, h = i >> 2, i & 3
+    pass_on(1)
+    pass_last(0)
+
+    def mix(b):
         rows = pl.ds(pl.multiple_of(b * 256, 256), 256)
-        lanes = pl.ds(pl.multiple_of(h * 128, 128), 128)
-        tok = dot_nn(wi[...], fo[h * 4 + b])
-        tok_out, tok_lse = tok[:, 0:128], tok[:, 128:256]
-        near_max = mx[rows, lanes]
-        top = jnp.maximum(near_max, tok_lse)
-        a = jnp.exp2(near_max - top)
-        b_far = jnp.exp2(tok_lse - top)
-        mixed = (num[rows, lanes] * a + tok_out * b_far) / (den[rows, lanes] * a + b_far)
-        att[rows, lanes] = mixed.astype(BF16)
-        return carry
-
-    lax.fori_loop(0, 16, mix, 0)
+
+        def one(h, carry):
+            lanes = pl.ds(pl.multiple_of(h * 128, 128), 128)
+            tok = dot_nn(wi[...], fo[h * 4 + b])
+            tok_out, tok_lse = tok[:, 0:128], tok[:, 128:256]
+            near_max = mx[rows, lanes]
+            top = jnp.maximum(near_max, tok_lse)
+            a = jnp.exp2(near_max - top)
+            b_far = jnp.exp2(tok_lse - top)
+            mixed = (num[rows, lanes] * a + tok_out * b_far) / (den[rows, lanes] * a + b_far)
+            att[rows, lanes] = mixed.astype(BF16)
+            return carry
+
+        lax.fori_loop(0, 4, one, 0)
+
+    def give(i):
+        row = pl.multiple_of((1 - half) * 512 + i * 256, 256)
+        return pltpu.make_async_remote_copy(
+            src_ref=att.at[pl.ds(row, 256)], dst_ref=att_in.at[i * 256 : i * 256 + 256],
+            send_sem=att_send.at[i], recv_sem=att_recv.at[i],
+            device_id={"head": partner}, device_id_type=MESH,
+        )
+
+    for i in range(2):
+        mix((1 - half) * 2 + i)
+        give(i).start()
+    pass_on(2)
+    pass_last(1)
+    for i in range(2):
+        mix(half * 2 + i)
+    load_w.wait()
+    for i in range(2):
+        give(i).wait_recv()
+
+    def share(target, chunk):
+        own_rows = pl.ds(pl.multiple_of(half * 512 + target * 128, 128), 128)
+        in_rows = pl.ds(pl.multiple_of(target * 128, 128), 128)
+        cols = pl.ds(pl.multiple_of(chunk * 512, 512), 512)
+        return dot_nn(att[own_rows, :], w_own[:, cols]) + dot_nn(att_in[in_rows, :], w_in[:, cols])
+
+    def first_copy(side, j):
+        slot = side * 4 + j
+        return pltpu.make_async_remote_copy(
+            src_ref=sb1.at[slot], dst_ref=rb1.at[slot], send_sem=send1.at[slot], recv_sem=recv1.at[slot],
+            device_id={"head": (up, down)[side]}, device_id_type=MESH,
+        )
+
+    def second_copy(side, chunk):
+        slot = side * 8 + chunk
+        return pltpu.make_async_remote_copy(
+            src_ref=sb2.at[slot], dst_ref=rb2.at[slot], send_sem=send2.at[slot], recv_sem=recv2.at[slot],
+            device_id={"head": (up, down)[side]}, device_id_type=MESH,
+        )
+
+    y_up, y_down, y_far = lax.rem(y + 1, 4), lax.rem(y + 3, 4), lax.rem(y + 2, 4)
+
+    def begin(j, carry):
+        w_sibling(j).wait_recv()
+        w_last(j).wait_recv()
+        for side in range(2):
+            sb1[side * 4 + j] = share(y_far, 2 * j + side).astype(BF16)
+            first_copy(side, j).start()
+        for side in range(2):
+            chunk = 2 * j + 1 - side
+            sb2[side * 8 + chunk] = share((y_up, y_down)[side], chunk).astype(BF16)
+            second_copy(side, chunk).start()
+        return carry
+
+    lax.fori_loop(0, 1, begin, 0)
+    pass_on(3)
+    pass_last(2)
+    lax.fori_loop(1, 2, begin, 0)
+    pass_last(3)
+    lax.fori_loop(2, 4, begin, 0)
+
+    def follow(j, carry):
+        for side in range(2):
+            chunk = 2 * j + side
+            mine = share((y_up, y_down)[side], chunk)
+            first_copy(side, j).wait_recv()
+            sb2[side * 8 + chunk] = (mine + rb1[side * 4 + j].astype(F32)).astype(BF16)
+            second_copy(side, chunk).start()
+        return carry
+
+    lax.fori_loop(0, 4, follow, 0)
+
+    def keep(chunk, carry):
+        own[chunk] = share(y, chunk)
+        return carry
+
+    lax.fori_loop(0, 8, keep, 0)
+
+    def finish(chunk, carry):
+        for side in range(2):
+            second_copy(side, chunk).wait_recv()
+        total = own[chunk] + rb2[chunk].astype(F32) + rb2[8 + chunk].astype(F32)
+        out[:, pl.ds(pl.multiple_of(chunk * 512, 512), 512)] = total.astype(BF16)
+        return carry
+
+    lax.fori_loop(0, 8, finish, 0)
 
     @pl.when(has_later(1))
     def _():
         copy_tail().wait_send()
 
     each(lambda copy: copy.wait_send(), has_later)
-
-
-def attention(n, q, k, v):
-    any_spec = pl.BlockSpec(memory_space=pl.ANY)
+    for j in range(4):
+        w_across(j).wait_send()
+        w_sibling(j).wait_send()
+        w_beside(j).wait_send()
+        w_last(j).wait_send()
+        for side in range(2):
+            first_copy(side, j).wait_send()
+            second_copy(side, j).wait_send()
+            second_copy(side, 4 + j).wait_send()
+    for i in range(2):
+        give(i).wait_send()
+
+
+def layer(n, q, k, v, w):
+    hbm_spec = pl.BlockSpec(memory_space=pltpu.HBM)
     vm = pltpu.VMEM
     return pl.pallas_call(
         functools.partial(kernel, n),
-        out_shape=jax.ShapeDtypeStruct(q.shape, BF16),
-        in_specs=[any_spec] * 3,
+        out_shape=jax.ShapeDtypeStruct((128, 4096), BF16),
+        in_specs=[hbm_spec] * 4,
         out_specs=pl.BlockSpec(memory_space=pltpu.VMEM),
         scratch_shapes=[
             vm((1280, 1024), BF16),
@@ -321,24 +463,30 @@
             vm((1024, 512), F32),
             vm((1024, 512), F32),
             vm((1024, 512), F32),
-            pltpu.SemaphoreType.DMA((3,)),
-            pltpu.SemaphoreType.DMA((35,)),
-            pltpu.SemaphoreType.DMA((35,)),
-        ],
+            vm((1024, 512), BF16),
+            vm((512, 512), BF16),
+            vm((512, 4096), BF16),
+            vm((512, 4096), BF16),
+            vm((8, 128, 512), BF16),
+            vm((8, 128, 512), BF16),
+            vm((16, 128, 512), BF16),
+            vm((16, 128, 512), BF16),
+            vm((8, 128, 512), F32),
+            pltpu.SemaphoreType.DMA((4,)),
+        ]
+        + [pltpu.SemaphoreType.DMA((count,)) for count in (35, 35, 2, 2, 16, 16, 8, 8, 16, 16)],
         compiler_params=pltpu.CompilerParams(
-            collective_id=0, has_side_effects=True, vmem_limit_bytes=48 * 1024 * 1024
+            collective_id=0, has_side_effects=True, vmem_limit_bytes=56 * 1024 * 1024
         ),
-        cost_estimate=pl.CostEstimate(flops=2 * 10**9, bytes_accessed=4 * 2**20, transcendentals=2 * 10**6),
-    )(q, k, v)
+        cost_estimate=pl.CostEstimate(flops=6 * 10**9, bytes_accessed=8 * 2**20, transcendentals=2 * 10**6),
+    )(q, k, v, w)
 
 
 def solution(mesh):
     n = mesh.shape["seq"]
 
     def body(queries, key_tokens, value_tokens, out_weight):
-        att = attention(n, queries, key_tokens, value_tokens)
-        share = jnp.dot(att, out_weight, preferred_element_type=F32).astype(BF16)
-        return lax.psum_scatter(share, "head", scatter_dimension=0, tiled=True)
+        return layer(n, queries, key_tokens, value_tokens, out_weight)
 
     in_specs = (P("seq", "head"), P("seq", "head"), P("seq", "head"), P("head", None))
     out_specs = P(("seq", "head"), None)

time: 181 us -> 92.8 us (0.51); the launches traced: 179 us -> 92.7 us
  waiting for transfers between devices: 121 us -> 0 us
  Pallas kernels: 33.8 us -> 90.4 us
  between operations: 13.4 us -> 0.01 us
  matrix products: 6.79 us -> 0 us
    reduce_scatter x1 -> x0, waiting for transfers between devices: 121 us -> none  [body(): return lax.psum_scatter(share, 'head', scatter_dimension=0, tiled=True)]
    pallas_call x1, Pallas kernels: 33.8 us -> 90.4 us  [layer(): pl.pallas_call(functools.partial(kernel, n), out_shape=jax.ShapeDtypeStru...]
    dot_general x1 -> x0, matrix products: 6.79 us -> none  [body(): share = jnp.dot(att, out_weight, preferred_element_type=F32).astype(BF16)]
    unnamed x8 -> x1, local copies, waits for them, and re-layouts: 3.68 us -> 2.29 us
  transfers between devices with their start and end apart: 1 -> 0, of which waited for: 1 -> 0; matrix products, arithmetic and copies ran while one was open for 0% -> 0% of each run, Pallas kernels for 0% -> 0%
where the time goes in v2:
time: 92.8 us; the launch traced here: 92.7 us
  Pallas kernels  90.4 us (97%)
  local copies, waits for them, and re-layouts  2.29 us (2%)
    pallas_call x1, Pallas kernels, layer(): pl.pallas_call(functools.partial(kernel, n), out_shape=jax.ShapeDtypeStru...  90.4 us
    unnamed x1, local copies, waits for them, and re-layouts  2.29 us

profile of v2, /device:TPU:34, one launch (start us, length us, event | category | flops | bytes accessed | tf_op | source)
XLA Modules:
  0.0 92.7 jit_solution(2082351680069381488)
XLA Ops:
  0.0 90.4 %shard_map.46 = bf16[128,4096]{1,0:T(8,128)(2,1)} custom-call(bf16[1024,512]{1,0:T(8,128)(2,1)} %q_hbm.1, bf16[1024,512]{1,0:T(8,128)(2,1)} %k_hbm.1, bf16[1024,512]{1,0:T(8,128)(2,1)} %v_hbm.1, bf16[512,4096]{1,0:T(8,128)(2,1)} %w_hbm.1), custom_call_target="tpu_custom_call" | custom-call | flops 6000000000 | bytes 8388608 | tf_op jit(solution)/shard_map/pallas_call | solution.py:444
  90.4 2.3 %copy.6 = bf16[128,4096]{1,0:T(8,128)(2,1)} copy(bf16[128,4096]{1,0:T(8,128)(2,1)} %shard_map.46) | data formatting | bytes 2097152

commit v3 on v2

v3 whole, which is shorter than its diff:
```python
import functools
import math

import jax
import jax.numpy as jnp
from jax import lax
from jax.experimental import pallas as pl
from jax.experimental.pallas import tpu as pltpu
from jax.sharding import PartitionSpec as P

MESH = pl.DeviceIdType.MESH
HD = 128
BLK = 256
QG = 16
LOG2E = 1.4426950408889634
SCALE2 = LOG2E / math.sqrt(HD)
BIG = -1e30
F32 = jnp.float32
BF16 = jnp.bfloat16

BACK3 = 6
STRIDE3 = 704


def iota(shape, dim):
    return lax.broadcasted_iota(jnp.int32, shape, dim)


def dot_nt(a, b):
    return lax.dot_general(a, b, (((1,), (1,)), ((), ())), preferred_element_type=F32)


def dot_nn(a, b):
    return jnp.dot(a, b, preferred_element_type=F32)


def fill_pool_matrix(pm):
    def piece(rows, shift, weight):
        hit = (iota((rows, 1024), 1) >> shift) == iota((rows, 1024), 0)
        return jnp.where(hit, weight, 0.0).astype(BF16)

    pm[0:128, :] = piece(128, 3, 1.0 / 8)
    pm[128:160, :] = piece(32, 5, 1.0 / 32)
    row, col = iota((16, 1024), 0), iota((16, 1024), 1)
    third = jnp.where((col >> 7) == row, 1.0 / 128, 0.0)
    fourth = jnp.where((col >> 9) == (row & 1), 1.0 / 512, 0.0)
    pm[160:176, :] = jnp.where(row < 8, third, fourth).astype(BF16)
    pm[176:240, :] = piece(64, 4, 1.0 / 16)


def fill_interp(wi):
    row, col = iota((BLK, 48), 0), iota((BLK, 48), 1)
    numer = 2 * row - (QG - 1)
    low = jnp.clip(numer >> 5, 0, BLK // QG - 2)
    frac = jnp.clip((numer - low * 32).astype(F32) * (1.0 / 32), 0.0, 1.0)
    group = col & 15
    value = jnp.where(group == low, 1.0 - frac, 0.0) + jnp.where(group == low + 1, frac, 0.0)
    wi[...] = value.astype(BF16)


def bounds(start):
    first = jnp.maximum(start - 256, 0)
    second = jnp.maximum(((first - 512) >> 5) << 5, 0)
    third = jnp.maximum(((second - 2048) >> 7) << 7, 0)
    fourth = jnp.maximum(((third - 8192) >> 9) << 9, 0)
    return first, second, third, fourth


def fill_masks(pick12, pick3, pick4, s0):
    shape = (64, 256)
    first, second, third, fourth = bounds(s0 + 256 * (iota(shape, 0) >> 4))
    col = iota(shape, 1)
    is_first = col < 160
    token = jnp.where(is_first, s0 - 768 + 8 * col, s0 - 3072 + 32 * (col - 160))
    size = jnp.where(is_first, 8, 32)
    lower = jnp.where(is_first, second, third)
    upper = jnp.where(is_first, first, second)
    pick12[...] = jnp.where((token >= lower) & (token + size <= upper), 1, 0)
    shape = (64, 384)
    first, second, third, fourth = bounds(s0 + 256 * (iota(shape, 0) >> 4))
    col = iota(shape, 1)
    core = jnp.where(col < 192, 0, 1)
    rest = col - 192 * core
    token = ((s0 >> 11) - BACK3 + (rest >> 5)) * 2048 + core * 1024 + (rest & 7) * 128
    chosen = (token >= fourth) & (token + 128 <= third)
    pick3[...] = jnp.where(chosen, (rest & 31) >> 3, -1)
    token = (rest >> 4) * 2048 + core * 1024 + (rest & 1) * 512
    chosen = (token >= 0) & (token + 512 <= fourth)
    pick4[...] = jnp.where(chosen, (rest & 15) >> 1, -1)


def kernel(
    n, q_hbm, k_hbm, v_hbm, w_hbm, out,
    kvx, qs, pm, wi, res, pool12, qp, far12, far3, far4, pick12, pick3, pick4, fo, num, mx, den,
    att, att_in, w_own, w_in, sb1, rb1, sb2, rb2, own,
    load_sem, near_send, near_recv, peer_send, peer_recv, side_send, side_recv,
    att_send, att_recv, w_send, w_recv, send1, recv1, send2, recv2,
):
    me = lax.axis_index("seq")
    head = lax.axis_index("head")
    s0 = me * 1024
    chips = n // 2
    row_chips = chips // 2
    core = lax.rem(me, 2)
    chip = lax.div(me, 2)
    x_low = lax.div(chip, row_chips)
    z = lax.rem(chip, row_chips)
    half = lax.div(head, 4)
    y = lax.rem(head, 4)
    partner = lax.rem(head + 4, 8)
    up = half * 4 + lax.rem(y + 1, 4)
    down = half * 4 + lax.rem(y + 3, 4)
    x_next = lax.rem(me + chips, n)
    across = {"seq": x_next, "head": partner}
    quarter = lax.rem(me, 4)
    sibling = me + 1 - 2 * core
    beside = me + 2 - 4 * lax.div(quarter, 2)

    def z_peer(d):
        return x_low * chips + lax.rem(z + d, row_chips) * 2 + core

    loads = [
        pltpu.make_async_copy(k_hbm, kvx.at[256:1280, 0:512], load_sem.at[0]),
        pltpu.make_async_copy(v_hbm, kvx.at[256:1280, 512:1024], load_sem.at[1]),
        pltpu.make_async_copy(q_hbm, qs, load_sem.at[2]),
    ]
    load_w = pltpu.make_async_copy(w_hbm, w_own, load_sem.at[3])
    for load in loads:
        load.start()

    for c in range(2):
        far3[c * STRIDE3 : c * STRIDE3 + BACK3 * 32, :] = jnp.zeros((BACK3 * 32, 256), BF16)
        far4[c * 256 + 128 : c * 256 + 256, :] = jnp.zeros((128, 256), BF16)

    barrier = pltpu.get_barrier_semaphore()
    places = [{"seq": z_peer(d)} for d in range(1, row_chips)]
    places += [{"seq": lax.rem(me + n - k, n)} for k in (1, 2, 3)]
    places += [{"seq": sibling}, {"seq": x_next}, {"head": partner}, {"head": up}, {"head": down}, across]
    for place in places:
        pl.semaphore_signal(barrier, inc=1, device_id=place, device_id_type=MESH)

    fill_pool_matrix(pm)
    for load in loads:
        load.wait()
    load_w.start()

    def pool(c, carry):
        cols = pl.ds(pl.multiple_of(c * 256, 256), 256)
        res[:, cols] = dot_nn(pm[0:176, :], kvx[256:1280, cols])
        return carry

    lax.fori_loop(0, 4, pool, 0)
    pool12[...] = res[0:160, :].astype(BF16)
    row8 = iota((8, 128), 0)
    sides3, sides4 = [], []
    for side in range(2):
        tiles = [res[160:168, side * 512 + h * 128 : side * 512 + (h + 1) * 128] for h in range(4)]
        last = jnp.zeros((8, 128), F32)
        for h in range(4):
            lanes = slice(side * 512 + h * 128, side * 512 + (h + 1) * 128)
            last = jnp.where((row8 >> 1) == h, res[168:176, lanes], last)
        sides3.append(jnp.concatenate(tiles, axis=0))
        sides4.append(jnp.concatenate([last, jnp.zeros((8, 128), F32)], axis=0))
    my3 = pl.ds(pl.multiple_of(core * STRIDE3 + (BACK3 + chip) * 32, 32), 32)
    my4 = pl.ds(pl.multiple_of(core * 256 + chip * 16, 16), 16)
    far3[my3, :] = jnp.concatenate(sides3, axis=1).astype(BF16)
    far4[my4, :] = jnp.concatenate(sides4, axis=1).astype(BF16)
    far12[96:160, :] = pool12[0:64, :]

    pl.semaphore_wait(barrier, len(places))

    def remote(src, dst, sends, recvs, slot, place):
        return pltpu.make_async_remote_copy(
            src_ref=src, dst_ref=dst, send_sem=sends.at[slot], recv_sem=recvs.at[slot],
            device_id=place, device_id_type=MESH,
        )

    def later(k):
        return {"seq": lax.rem(me + k, n)}

    def row2(k):
        return 160 + 32 * (3 - k)

    near_copies = [
        remote(pool12.at[128:160], far12.at[row2(k) : row2(k) + 32], near_send, near_recv, k - 1, later(k))
        for k in (1, 2, 3)
    ]
    near_copies.append(remote(pool12.at[32:128], far12.at[0:96], near_send, near_recv, 3, later(1)))
    tail_copy = remote(kvx.at[1024:1280], kvx.at[0:256], near_send, near_recv, 4, later(1))

    def peer_copies(d):
        return (
            remote(far3.at[my3], far3.at[my3], peer_send, peer_recv, d, {"seq": z_peer(d)}),
            remote(far4.at[my4], far4.at[my4], peer_send, peer_recv, 8 + d, {"seq": z_peer(d)}),
        )

    def line_copies(x, slot, place):
        rows3 = pl.ds(pl.multiple_of(core * STRIDE3 + (BACK3 + x * row_chips) * 32, 32), row_chips * 32)
        rows4 = pl.ds(pl.multiple_of(core * 256 + x * 128, 128), row_chips * 16)
        return (
            remote(far3.at[rows3], far3.at[rows3], side_send, side_recv, slot, place),
            remote(far4.at[rows4], far4.at[rows4], side_send, side_recv, slot + 1, place),
        )

    line_sibling = line_copies(x_low, 0, {"seq": sibling})
    line_next = line_copies(0, 2, {"seq": x_next})
    line_last = line_copies(0, 4, {"seq": sibling})

    for d in range(1, row_chips):
        for copy in peer_copies(d):
            copy.start()
    for copy in near_copies:
        copy.start()
    tail_copy.start()

    def w_copy(src, kind, j, rows_of, place):
        rows = pl.ds(pl.multiple_of(rows_of * 128, 128), 128)
        cols = pl.ds(pl.multiple_of(j * 1024, 1024), 1024)
        return remote(src.at[rows, cols], w_in.at[rows, cols], w_send, w_recv, kind * 4 + j, place)

    other = lax.rem(quarter + 2, 4)
    w_across = lambda j: w_copy(w_hbm, 0, j, quarter, across)
    w_sibling = lambda j: w_copy(w_in, 1, j, quarter, {"seq": sibling})
    w_beside = lambda j: w_copy(w_in, 2, j, quarter, {"seq": beside})
    w_last = lambda j: w_copy(w_in, 3, j, other, {"seq": sibling})

    def pass_on(j):
        w_across(j).wait_recv()
        w_sibling(j).start()
        w_beside(j).start()

    def pass_last(j):
        w_beside(j).wait_recv()
        w_last(j).start()

    for j in range(4):
        w_across(j).start()

    qp[...] = dot_nn(pm[176:240, :], qs[...]).astype(BF16)
    fill_interp(wi)
    fill_masks(pick12, pick3, pick4, s0)

    def near(b, h):
        rows = pl.ds(pl.multiple_of(b * 256, 256), 256)
        next_rows = pl.ds(pl.multiple_of(b * 256 + 256, 256), 256)
        lanes = pl.ds(pl.multiple_of(h * 128, 128), 128)
        vlanes = pl.ds(pl.multiple_of(512 + h * 128, 128), 128)
        q = qs[rows, lanes]
        s_prev = dot_nt(q, kvx[rows, lanes])
        s_own = dot_nt(q, kvx[next_rows, lanes])
        s_prev = jnp.where(s0 + b * 256 > 0, s_prev, BIG)
        s_own = jnp.where(iota((256, 256), 1) <= iota((256, 256), 0), s_own, BIG)
        top = jnp.max(jnp.maximum(s_prev, s_own), axis=1, keepdims=True) * SCALE2
        w_prev = jnp.exp2(s_prev * SCALE2 - top)
        w_own = jnp.exp2(s_own * SCALE2 - top)
        total = jnp.sum(w_prev + w_own, axis=1, keepdims=True)
        num[rows, lanes] = dot_nn(w_prev.astype(BF16), kvx[rows, vlanes]) + dot_nn(
            w_own.astype(BF16), kvx[next_rows, vlanes]
        )
        mx[rows, lanes] = jnp.broadcast_to(top, (256, 128))
        den[rows, lanes] = jnp.broadcast_to(total, (256, 128))

    def near_step(i, carry):
        near(i >> 2, i & 3)
        return carry

    lax.fori_loop(4, 12, near_step, 0)
    for d in range(1, row_chips):
        for copy in peer_copies(d):
            copy.wait_recv()
    for copy in line_sibling:
        copy.start()

    @pl.when(x_low == 0)
    def _():
        for copy in line_next:
            copy.start()

    lax.fori_loop(12, 16, near_step, 0)

    @pl.when(x_low == 1)
    def _():
        for copy in line_next:
            copy.wait_recv()
        for copy in line_last:
            copy.start()

    for copy in line_sibling:
        copy.wait_recv()
    for copy in near_copies:
        copy.wait_recv()

    @pl.when(x_low == 1)
    def _():
        for copy in line_last:
            copy.wait_recv()

    windows3 = [pl.ds(pl.multiple_of(c * STRIDE3 + chip * 32, 32), 192) for c in range(2)]
    windows4 = [pl.ds(c * 256, 192) for c in range(2)]

    def two(ref, windows, lanes):
        return jnp.concatenate([ref[w, lanes] for w in windows], axis=0)

    def far(h, carry):
        lanes = pl.ds(pl.multiple_of(h * 128, 128), 128)
        vlanes = pl.ds(pl.multiple_of(512 + h * 128, 128), 128)
        keys, values = slice(0, 128), slice(128, 256)
        pooled = qp[:, lanes]
        parts = [
            (pick12[...] > 0, far12[:, lanes], far12[:, vlanes]),
            (pick3[...] == h, two(far3, windows3, keys), two(far3, windows3, values)),
            (pick4[...] == h, two(far4, windows4, keys), two(far4, windows4, values)),
        ]
        scores = [jnp.where(chosen, dot_nt(pooled, key), BIG) for chosen, key, _ in parts]
        top = functools.reduce(jnp.maximum, [jnp.max(s, axis=1, keepdims=True) for s in scores]) * SCALE2
        weights = [
            jnp.where(chosen, jnp.exp2(s * SCALE2 - top), 0.0) for (chosen, _, _), s in zip(parts, scores)
        ]
        total = sum(jnp.sum(w, axis=1, keepdims=True) for w in weights)
        acc = sum(dot_nn(w.astype(BF16), value) for w, (_, _, value) in zip(weights, parts))
        some = total > 0
        safe = jnp.where(some, total, 1.0)
        lse = jnp.where(some, top + jnp.log(safe) * LOG2E, BIG)
        both = jnp.concatenate([acc / safe, jnp.broadcast_to(lse, (64, 128))], axis=1)
        high = both.astype(BF16)
        rest = both - high.astype(F32)
        middle = rest.astype(BF16)
        low = (rest - middle.astype(F32)).astype(BF16)
        for b in range(4):
            for j, part in enumerate((high, middle, low)):
                fo[h * 4 + b, 16 * j : 16 * (j + 1), :] = part[16 * b : 16 * (b + 1), :]
        return carry

    lax.fori_loop(0, 4, far, 0)

    tail_copy.wait_recv()
    lax.fori_loop(0, 4, near_step, 0)
    pass_on(0)
    pass_on(1)

    y_up, y_down, y_far = lax.rem(y + 1, 4), lax.rem(y + 3, 4), lax.rem(y + 2, 4)
    order = [y_far, y_up, y_down, y]

    def mix(row):
        rows = pl.ds(pl.multiple_of(row, 128), 128)
        b = lax.div(row, 256)
        weights = wi[pl.ds(pl.multiple_of(lax.rem(row, 256), 128), 128), :]

        def one(h, carry):
            lanes = pl.ds(pl.multiple_of(h * 128, 128), 128)
            tok = dot_nn(weights, fo[h * 4 + b])
            tok_out, tok_lse = tok[:, 0:128], tok[:, 128:256]
            near_max = mx[rows, lanes]
            top = jnp.maximum(near_max, tok_lse)
            a = jnp.exp2(near_max - top)
            b_far = jnp.exp2(tok_lse - top)
            mixed = (num[rows, lanes] * a + tok_out * b_far) / (den[rows, lanes] * a + b_far)
            att[rows, lanes] = mixed.astype(BF16)
            return carry

        lax.fori_loop(0, 4, one, 0)

    def give(i):
        target = order[i]
        src = pl.ds(pl.multiple_of((1 - half) * 512 + target * 128, 128), 128)
        dst = pl.ds(pl.multiple_of(target * 128, 128), 128)
        return remote(att.at[src], att_in.at[dst], att_send, att_recv, i, {"head": partner})

    def mix_out(i):
        mix((1 - half) * 512 + order[i] * 128)
        give(i).start()

    def mix_own(i):
        mix(half * 512 + order[i] * 128)

    mix_out(0)
    mix_out(1)
    mix_out(2)
    mix_own(0)
    pass_on(2)
    pass_last(0)
    mix_out(3)
    for i in (1, 2, 3):
        mix_own(i)
    pass_on(3)
    pass_last(1)
    load_w.wait()

    def share(target, chunk):
        own_rows = pl.ds(pl.multiple_of(half * 512 + target * 128, 128), 128)
        in_rows = pl.ds(pl.multiple_of(target * 128, 128), 128)
        cols = pl.ds(pl.multiple_of(chunk * 512, 512), 512)
        return dot_nn(att[own_rows, :], w_own[:, cols]) + dot_nn(att_in[in_rows, :], w_in[:, cols])

    def first_copy(side, j):
        slot = side * 4 + j
        return remote(sb1.at[slot], rb1.at[slot], send1, recv1, slot, {"head": (up, down)[side]})

    def second_copy(side, chunk):
        slot = side * 8 + chunk
        return remote(sb2.at[slot], rb2.at[slot], send2, recv2, slot, {"head": (up, down)[side]})

    def begin(j, carry):
        w_sibling(j).wait_recv()
        w_last(j).wait_recv()
        for side in range(2):
            sb1[side * 4 + j] = share(y_far, 2 * j + side).astype(BF16)
            first_copy(side, j).start()
        return carry

    def direct(j, carry):
        for side in range(2):
            chunk = 2 * j + 1 - side
            sb2[side * 8 + chunk] = share((y_up, y_down)[side], chunk).astype(BF16)
            second_copy(side, chunk).start()
        return carry

    give(0).wait_recv()
    lax.fori_loop(0, 2, begin, 0)
    give(1).wait_recv()
    give(2).wait_recv()
    lax.fori_loop(0, 2, direct, 0)
    pass_last(2)
    pass_last(3)

    def both(j, carry):
        begin(j, carry)
        return direct(j, carry)

    lax.fori_loop(2, 4, both, 0)

    def follow(j, carry):
        for side in range(2):
            chunk = 2 * j + side
            mine = share((y_up, y_down)[side], chunk)
            first_copy(side, j).wait_recv()
            sb2[side * 8 + chunk] = (mine + rb1[side * 4 + j].astype(F32)).astype(BF16)
            second_copy(side, chunk).start()
        return carry

    lax.fori_loop(0, 4, follow, 0)

    give(3).wait_recv()

    def keep(chunk, carry):
        own[chunk] = share(y, chunk)
        return carry

    lax.fori_loop(0, 8, keep, 0)

    def finish(chunk, carry):
        for side in range(2):
            second_copy(side, chunk).wait_recv()
        total = own[chunk] + rb2[chunk].astype(F32) + rb2[8 + chunk].astype(F32)
        out[:, pl.ds(pl.multiple_of(chunk * 512, 512), 512)] = total.astype(BF16)
        return carry

    lax.fori_loop(0, 8, finish, 0)

    for d in range(1, row_chips):
        for copy in peer_copies(d):
            copy.wait_send()
    for copy in near_copies + [tail_copy] + list(line_sibling):
        copy.wait_send()

    @pl.when(x_low == 0)
    def _():
        for copy in line_next:
            copy.wait_send()

    @pl.when(x_low == 1)
    def _():
        for copy in line_last:
            copy.wait_send()

    for j in range(4):
        w_across(j).wait_send()
        w_sibling(j).wait_send()
        w_beside(j).wait_send()
        w_last(j).wait_send()
        for side in range(2):
            first_copy(side, j).wait_send()
            second_copy(side, j).wait_send()
            second_copy(side, 4 + j).wait_send()
    for i in range(4):
        give(i).wait_send()


def layer(n, q, k, v, w):
    hbm_spec = pl.BlockSpec(memory_space=pltpu.HBM)
    vm = pltpu.VMEM
    return pl.pallas_call(
        functools.partial(kernel, n),
        out_shape=jax.ShapeDtypeStruct((128, 4096), BF16),
        in_specs=[hbm_spec] * 4,
        out_specs=pl.BlockSpec(memory_space=pltpu.VMEM),
        scratch_shapes=[
            vm((1280, 1024), BF16),
            vm((1024, 512), BF16),
            vm((240, 1024), BF16),
            vm((256, 48), BF16),
            vm((176, 1024), F32),
            vm((160, 1024), BF16),
            vm((64, 512), BF16),
            vm((256, 1024), BF16),
            vm((2 * STRIDE3, 256), BF16),
            vm((512, 256), BF16),
            vm((64, 256), jnp.int32),
            vm((64, 384), jnp.int32),
            vm((64, 384), jnp.int32),
            vm((16, 48, 256), BF16),
            vm((1024, 512), F32),
            vm((1024, 512), F32),
            vm((1024, 512), F32),
            vm((1024, 512), BF16),
            vm((512, 512), BF16),
            vm((512, 4096), BF16),
            vm((512, 4096), BF16),
            vm((8, 128, 512), BF16),
            vm((8, 128, 512), BF16),
            vm((16, 128, 512), BF16),
            vm((16, 128, 512), BF16),
            vm((8, 128, 512), F32),
            pltpu.SemaphoreType.DMA((4,)),
        ]
        + [pltpu.SemaphoreType.DMA((count,)) for count in (5, 5, 16, 16, 6, 6, 4, 4, 16, 16, 8, 8, 16, 16)],
        compiler_params=pltpu.CompilerParams(
            collective_id=0, has_side_effects=True, vmem_limit_bytes=56 * 1024 * 1024
        ),
        cost_estimate=pl.CostEstimate(flops=6 * 10**9, bytes_accessed=8 * 2**20, transcendentals=2 * 10**6),
    )(q, k, v, w)


def solution(mesh):
    n = mesh.shape["seq"]

    def body(queries, key_tokens, value_tokens, out_weight):
        return layer(n, queries, key_tokens, value_tokens, out_weight)

    in_specs = (P("seq", "head"), P("seq", "head"), P("seq", "head"), P("head", None))
    out_specs = P(("seq", "head"), None)
    return jax.shard_map(body, mesh=mesh, in_specs=in_specs, out_specs=out_specs, check_vma=False)
```

time: 92.8 us -> 90 us (0.970)
  Pallas kernels: 90.4 us -> 87.1 us
    pallas_call x1, Pallas kernels: 90.4 us -> 87.1 us  [layer(): pl.pallas_call(functools.partial(kernel, n), out_shape=jax.ShapeDtypeStru...]
where the time goes in v3:
time: 90 us; the launch traced here: 89.4 us
  Pallas kernels  87.1 us (97%)
  local copies, waits for them, and re-layouts  2.29 us (3%)
    pallas_call x1, Pallas kernels, layer(): pl.pallas_call(functools.partial(kernel, n), out_shape=jax.ShapeDtypeStru...  87.1 us
    unnamed x1, local copies, waits for them, and re-layouts  2.29 us

profile of v3, /device:TPU:34, one launch (start us, length us, event | category | flops | bytes accessed | tf_op | source)
XLA Modules:
  0.0 89.4 jit_solution(5686722146743403693)
XLA Ops:
  0.0 87.1 %shard_map.46 = bf16[128,4096]{1,0:T(8,128)(2,1)} custom-call(bf16[1024,512]{1,0:T(8,128)(2,1)} %q_hbm.1, bf16[1024,512]{1,0:T(8,128)(2,1)} %k_hbm.1, bf16[1024,512]{1,0:T(8,128)(2,1)} %v_hbm.1, bf16[512,4096]{1,0:T(8,128)(2,1)} %w_hbm.1), custom_call_target="tpu_custom_call" | custom-call | flops 6000000000 | bytes 8388608 | tf_op jit(solution)/shard_map/pallas_call | solution.py:492
  87.1 2.3 %copy.6 = bf16[128,4096]{1,0:T(8,128)(2,1)} copy(bf16[128,4096]{1,0:T(8,128)(2,1)} %shard_map.46) | data formatting | bytes 2097152

commit v4 on v3

--- a/solution.py
+++ b/solution.py
@@ -90,11 +90,11 @@
 
 
 def kernel(
-    n, q_hbm, k_hbm, v_hbm, w_hbm, out,
+    n, q_hbm, k_hbm, v_hbm, w_hbm, result,
     kvx, qs, pm, wi, res, pool12, qp, far12, far3, far4, pick12, pick3, pick4, fo, num, mx, den,
-    att, att_in, w_own, w_in, sb1, rb1, sb2, rb2, own,
+    att, att_in, w_own, w_in, sb1, rb1, sb2, rb2, own, out,
     load_sem, near_send, near_recv, peer_send, peer_recv, side_send, side_recv,
-    att_send, att_recv, w_send, w_recv, send1, recv1, send2, recv2,
+    att_send, att_recv, w_send, w_recv, send1, recv1, send2, recv2, out_sem,
 ):
     me = lax.axis_index("seq")
     head = lax.axis_index("head")
@@ -112,44 +112,92 @@
     down = half * 4 + lax.rem(y + 3, 4)
     x_next = lax.rem(me + chips, n)
     across = {"seq": x_next, "head": partner}
-    quarter = lax.rem(me, 4)
+    side_x = x_low * 2 + core
+    side_z = lax.rem(me, 4)
+    beside_z = me + 2 - 4 * lax.div(side_z, 2)
     sibling = me + 1 - 2 * core
-    beside = me + 2 - 4 * lax.div(quarter, 2)
 
     def z_peer(d):
         return x_low * chips + lax.rem(z + d, row_chips) * 2 + core
 
-    loads = [
-        pltpu.make_async_copy(k_hbm, kvx.at[256:1280, 0:512], load_sem.at[0]),
-        pltpu.make_async_copy(v_hbm, kvx.at[256:1280, 512:1024], load_sem.at[1]),
-        pltpu.make_async_copy(q_hbm, qs, load_sem.at[2]),
-    ]
-    load_w = pltpu.make_async_copy(w_hbm, w_own, load_sem.at[3])
-    for load in loads:
-        load.start()
-
+    barrier = pltpu.get_barrier_semaphore()
     for c in range(2):
         far3[c * STRIDE3 : c * STRIDE3 + BACK3 * 32, :] = jnp.zeros((BACK3 * 32, 256), BF16)
         far4[c * 256 + 128 : c * 256 + 256, :] = jnp.zeros((128, 256), BF16)
-
-    barrier = pltpu.get_barrier_semaphore()
     places = [{"seq": z_peer(d)} for d in range(1, row_chips)]
-    places += [{"seq": lax.rem(me + n - k, n)} for k in (1, 2, 3)]
+    places += [{"seq": lax.rem(me + n - k, n)} for k in (1, 2, 3 - 2 * core)]
     places += [{"seq": sibling}, {"seq": x_next}, {"head": partner}, {"head": up}, {"head": down}, across]
     for place in places:
         pl.semaphore_signal(barrier, inc=1, device_id=place, device_id_type=MESH)
 
+    load_k = pltpu.make_async_copy(k_hbm, kvx.at[256:1280, 0:512], load_sem.at[0])
+    load_v = pltpu.make_async_copy(v_hbm, kvx.at[256:1280, 512:1024], load_sem.at[1])
+    load_q = pltpu.make_async_copy(q_hbm, qs, load_sem.at[2])
+    load_w = pltpu.make_async_copy(w_hbm, w_own, load_sem.at[3])
+    load_k.start()
+    load_v.start()
+    load_q.start()
+
+    def remote(src, dst, sends, recvs, slot, place):
+        return pltpu.make_async_remote_copy(
+            src_ref=src, dst_ref=dst, send_sem=sends.at[slot], recv_sem=recvs.at[slot],
+            device_id=place, device_id_type=MESH,
+        )
+
+    def later(k):
+        return {"seq": lax.rem(me + k, n)}
+
+    def w_copy(src, kind, j, rows_of, place):
+        rows = pl.ds(pl.multiple_of(rows_of * 128, 128), 128)
+        cols = pl.ds(pl.multiple_of(j * 1024, 1024), 1024)
+        return remote(src.at[rows, cols], w_in.at[rows, cols], w_send, w_recv, kind * 4 + j, place)
+
+    def place_of(j):
+        if j < 2:
+            return side_x, lax.rem(side_x + 2, 4), x_next
+        return side_z, side_z, beside_z
+
+    def w_across(j):
+        return w_copy(w_hbm, 0, j, place_of(j)[1], across)
+
+    def w_sibling(j):
+        return w_copy(w_in, 1, j, place_of(j)[0], {"seq": sibling})
+
+    def w_beside(j):
+        return w_copy(w_in, 2, j, place_of(j)[0], {"seq": place_of(j)[2]})
+
+    def w_last(j):
+        return w_copy(w_in, 3, j, lax.rem(place_of(j)[0] + 2, 4), {"seq": sibling})
+
+    def pass_on(j):
+        w_across(j).wait_recv()
+        w_sibling(j).start()
+        w_beside(j).start()
+
+    def pass_last(j):
+        w_beside(j).wait_recv()
+        w_last(j).start()
+
+    tail_copies = [
+        remote(ref.at[768:1024], kvx.at[0:256, i * 512 : i * 512 + 512], near_send, near_recv, 4 + i, later(1))
+        for i, ref in enumerate((k_hbm, v_hbm))
+    ]
+
     fill_pool_matrix(pm)
-    for load in loads:
-        load.wait()
-    load_w.start()
+    pl.semaphore_wait(barrier, len(places))
+    for copy in tail_copies:
+        copy.start()
+    w_across(0).start()
 
     def pool(c, carry):
         cols = pl.ds(pl.multiple_of(c * 256, 256), 256)
         res[:, cols] = dot_nn(pm[0:176, :], kvx[256:1280, cols])
         return carry
 
-    lax.fori_loop(0, 4, pool, 0)
+    load_k.wait()
+    lax.fori_loop(0, 2, pool, 0)
+    load_v.wait()
+    lax.fori_loop(2, 4, pool, 0)
     pool12[...] = res[0:160, :].astype(BF16)
     row8 = iota((8, 128), 0)
     sides3, sides4 = [], []
@@ -167,27 +215,17 @@
     far4[my4, :] = jnp.concatenate(sides4, axis=1).astype(BF16)
     far12[96:160, :] = pool12[0:64, :]
 
-    pl.semaphore_wait(barrier, len(places))
-
-    def remote(src, dst, sends, recvs, slot, place):
-        return pltpu.make_async_remote_copy(
-            src_ref=src, dst_ref=dst, send_sem=sends.at[slot], recv_sem=recvs.at[slot],
-            device_id=place, device_id_type=MESH,
-        )
-
-    def later(k):
-        return {"seq": lax.rem(me + k, n)}
-
-    def row2(k):
-        return 160 + 32 * (3 - k)
-
+    def rows2(row):
+        return far12.at[pl.ds(pl.multiple_of(row, 32), 32)]
+
+    own2 = pool12.at[128:160]
+    second_far = 1 + 2 * core
     near_copies = [
-        remote(pool12.at[128:160], far12.at[row2(k) : row2(k) + 32], near_send, near_recv, k - 1, later(k))
-        for k in (1, 2, 3)
+        remote(own2, rows2(192), near_send, near_recv, 0, later(2)),
+        remote(own2, rows2(224 - 64 * core), near_send, near_recv, 1, later(second_far)),
+        remote(pool12.at[32:128], far12.at[0:96], near_send, near_recv, 2, later(1)),
     ]
-    near_copies.append(remote(pool12.at[32:128], far12.at[0:96], near_send, near_recv, 3, later(1)))
-    tail_copy = remote(kvx.at[1024:1280], kvx.at[0:256], near_send, near_recv, 4, later(1))
-
+    pass2 = remote(rows2(192), rows2(160 + 64 * core), near_send, near_recv, 3, {"seq": sibling})
     def peer_copies(d):
         return (
             remote(far3.at[my3], far3.at[my3], peer_send, peer_recv, d, {"seq": z_peer(d)}),
@@ -211,30 +249,8 @@
             copy.start()
     for copy in near_copies:
         copy.start()
-    tail_copy.start()
-
-    def w_copy(src, kind, j, rows_of, place):
-        rows = pl.ds(pl.multiple_of(rows_of * 128, 128), 128)
-        cols = pl.ds(pl.multiple_of(j * 1024, 1024), 1024)
-        return remote(src.at[rows, cols], w_in.at[rows, cols], w_send, w_recv, kind * 4 + j, place)
-
-    other = lax.rem(quarter + 2, 4)
-    w_across = lambda j: w_copy(w_hbm, 0, j, quarter, across)
-    w_sibling = lambda j: w_copy(w_in, 1, j, quarter, {"seq": sibling})
-    w_beside = lambda j: w_copy(w_in, 2, j, quarter, {"seq": beside})
-    w_last = lambda j: w_copy(w_in, 3, j, other, {"seq": sibling})
-
-    def pass_on(j):
-        w_across(j).wait_recv()
-        w_sibling(j).start()
-        w_beside(j).start()
-
-    def pass_last(j):
-        w_beside(j).wait_recv()
-        w_last(j).start()
-
-    for j in range(4):
-        w_across(j).start()
+    load_q.wait()
+    load_w.start()
 
     qp[...] = dot_nn(pm[176:240, :], qs[...]).astype(BF16)
     fill_interp(wi)
@@ -253,18 +269,22 @@
         top = jnp.max(jnp.maximum(s_prev, s_own), axis=1, keepdims=True) * SCALE2
         w_prev = jnp.exp2(s_prev * SCALE2 - top)
         w_own = jnp.exp2(s_own * SCALE2 - top)
-        total = jnp.sum(w_prev + w_own, axis=1, keepdims=True)
-        num[rows, lanes] = dot_nn(w_prev.astype(BF16), kvx[rows, vlanes]) + dot_nn(
-            w_own.astype(BF16), kvx[next_rows, vlanes]
-        )
+        ones = jnp.ones((256, 128), BF16)
+        acc = dot_nn(w_prev.astype(BF16), jnp.concatenate([kvx[rows, vlanes], ones], axis=1))
+        acc += dot_nn(w_own.astype(BF16), jnp.concatenate([kvx[next_rows, vlanes], ones], axis=1))
+        num[rows, lanes] = acc[:, 0:128]
+        den[rows, lanes] = acc[:, 128:256]
         mx[rows, lanes] = jnp.broadcast_to(top, (256, 128))
-        den[rows, lanes] = jnp.broadcast_to(total, (256, 128))
 
     def near_step(i, carry):
-        near(i >> 2, i & 3)
-        return carry
-
-    lax.fori_loop(4, 12, near_step, 0)
+        near(i >> 1, (i & 1) * 2)
+        near(i >> 1, (i & 1) * 2 + 1)
+        return carry
+
+    w_across(1).start()
+    lax.fori_loop(2, 5, near_step, 0)
+    pass_on(0)
+    lax.fori_loop(5, 6, near_step, 0)
     for d in range(1, row_chips):
         for copy in peer_copies(d):
             copy.wait_recv()
@@ -276,7 +296,15 @@
         for copy in line_next:
             copy.start()
 
-    lax.fori_loop(12, 16, near_step, 0)
+    near_copies[0].wait_recv()
+    pass2.start()
+    w_across(2).start()
+    lax.fori_loop(6, 8, near_step, 0)
+    for copy in tail_copies:
+        copy.wait_recv()
+    lax.fori_loop(0, 2, near_step, 0)
+    pass_on(1)
+    w_across(3).start()
 
     @pl.when(x_low == 1)
     def _():
@@ -285,9 +313,10 @@
         for copy in line_last:
             copy.start()
 
+    pass_last(0)
     for copy in line_sibling:
         copy.wait_recv()
-    for copy in near_copies:
+    for copy in near_copies[1:] + [pass2]:
         copy.wait_recv()
 
     @pl.when(x_low == 1)
@@ -301,9 +330,9 @@
     def two(ref, windows, lanes):
         return jnp.concatenate([ref[w, lanes] for w in windows], axis=0)
 
-    def far(h, carry):
-        lanes = pl.ds(pl.multiple_of(h * 128, 128), 128)
-        vlanes = pl.ds(pl.multiple_of(512 + h * 128, 128), 128)
+    def far(h):
+        lanes = slice(h * 128, h * 128 + 128)
+        vlanes = slice(512 + h * 128, 640 + h * 128)
         keys, values = slice(0, 128), slice(128, 256)
         pooled = qp[:, lanes]
         parts = [
@@ -329,25 +358,21 @@
         for b in range(4):
             for j, part in enumerate((high, middle, low)):
                 fo[h * 4 + b, 16 * j : 16 * (j + 1), :] = part[16 * b : 16 * (b + 1), :]
-        return carry
-
-    lax.fori_loop(0, 4, far, 0)
-
-    tail_copy.wait_recv()
-    lax.fori_loop(0, 4, near_step, 0)
-    pass_on(0)
-    pass_on(1)
+
+    for h in range(4):
+        far(h)
+    pass_on(2)
+    pass_last(1)
 
     y_up, y_down, y_far = lax.rem(y + 1, 4), lax.rem(y + 3, 4), lax.rem(y + 2, 4)
-    order = [y_far, y_up, y_down, y]
 
     def mix(row):
         rows = pl.ds(pl.multiple_of(row, 128), 128)
         b = lax.div(row, 256)
         weights = wi[pl.ds(pl.multiple_of(lax.rem(row, 256), 128), 128), :]
 
-        def one(h, carry):
-            lanes = pl.ds(pl.multiple_of(h * 128, 128), 128)
+        for h in range(4):
+            lanes = slice(h * 128, h * 128 + 128)
             tok = dot_nn(weights, fo[h * 4 + b])
             tok_out, tok_lse = tok[:, 0:128], tok[:, 128:256]
             near_max = mx[rows, lanes]
@@ -356,34 +381,28 @@
             b_far = jnp.exp2(tok_lse - top)
             mixed = (num[rows, lanes] * a + tok_out * b_far) / (den[rows, lanes] * a + b_far)
             att[rows, lanes] = mixed.astype(BF16)
-            return carry
-
-        lax.fori_loop(0, 4, one, 0)
-
-    def give(i):
-        target = order[i]
+
+    def give(target):
         src = pl.ds(pl.multiple_of((1 - half) * 512 + target * 128, 128), 128)
         dst = pl.ds(pl.multiple_of(target * 128, 128), 128)
-        return remote(att.at[src], att_in.at[dst], att_send, att_recv, i, {"head": partner})
-
-    def mix_out(i):
-        mix((1 - half) * 512 + order[i] * 128)
-        give(i).start()
-
-    def mix_own(i):
-        mix(half * 512 + order[i] * 128)
-
-    mix_out(0)
-    mix_out(1)
-    mix_out(2)
-    mix_own(0)
-    pass_on(2)
-    pass_last(0)
-    mix_out(3)
-    for i in (1, 2, 3):
-        mix_own(i)
-    pass_on(3)
-    pass_last(1)
+        return remote(att.at[src], att_in.at[dst], att_send, att_recv, target, {"head": partner})
+
+    def mix_out(target):
+        mix((1 - half) * 512 + target * 128)
+
+    def mix_own(target):
+        mix(half * 512 + target * 128)
+
+    mix_out(y_far)
+    give(y_far).start()
+    mix_own(y_far)
+    mix_out(y_up)
+    give(y_up).start()
+    mix_out(y_down)
+    mix_own(y_up)
+    mix_own(y_down)
+    mix_out(y)
+    mix_own(y)
     load_w.wait()
 
     def share(target, chunk):
@@ -400,34 +419,56 @@
         slot = side * 8 + chunk
         return remote(sb2.at[slot], rb2.at[slot], send2, recv2, slot, {"head": (up, down)[side]})
 
-    def begin(j, carry):
+    def w_ready(j):
         w_sibling(j).wait_recv()
         w_last(j).wait_recv()
+
+    def begin(j, carry):
         for side in range(2):
             sb1[side * 4 + j] = share(y_far, 2 * j + side).astype(BF16)
             first_copy(side, j).start()
         return carry
 
-    def direct(j, carry):
-        for side in range(2):
-            chunk = 2 * j + 1 - side
-            sb2[side * 8 + chunk] = share((y_up, y_down)[side], chunk).astype(BF16)
-            second_copy(side, chunk).start()
-        return carry
-
-    give(0).wait_recv()
-    lax.fori_loop(0, 2, begin, 0)
-    give(1).wait_recv()
-    give(2).wait_recv()
-    lax.fori_loop(0, 2, direct, 0)
-    pass_last(2)
-    pass_last(3)
+    def direct(side, j):
+        chunk = 2 * j + 1 - side
+        sb2[side * 8 + chunk] = share((y_up, y_down)[side], chunk).astype(BF16)
+        second_copy(side, chunk).start()
+
+    def direct_up(j, carry):
+        direct(0, j)
+        return carry
+
+    def direct_down(j, carry):
+        direct(1, j)
+        return carry
 
     def both(j, carry):
         begin(j, carry)
-        return direct(j, carry)
-
-    lax.fori_loop(2, 4, both, 0)
+        direct(0, j)
+        direct(1, j)
+        return carry
+
+    give(y_far).wait_send()
+    give(y_down).start()
+    give(y_far).wait_recv()
+    w_ready(0)
+    lax.fori_loop(0, 1, begin, 0)
+    pass_on(3)
+    w_ready(1)
+    lax.fori_loop(1, 2, begin, 0)
+    give(y_up).wait_send()
+    give(y).start()
+    give(y_up).wait_recv()
+    lax.fori_loop(0, 2, direct_up, 0)
+    give(y_down).wait_send()
+    give(y_down).wait_recv()
+    lax.fori_loop(0, 2, direct_down, 0)
+    pass_last(2)
+    w_ready(2)
+    lax.fori_loop(2, 3, both, 0)
+    pass_last(3)
+    w_ready(3)
+    lax.fori_loop(3, 4, both, 0)
 
     def follow(j, carry):
         for side in range(2):
@@ -440,19 +481,24 @@
 
     lax.fori_loop(0, 4, follow, 0)
 
-    give(3).wait_recv()
+    give(y).wait_recv()
 
     def keep(chunk, carry):
         own[chunk] = share(y, chunk)
         return carry
 
     lax.fori_loop(0, 8, keep, 0)
+
+    def store(chunk):
+        cols = pl.ds(pl.multiple_of(chunk * 512, 512), 512)
+        return pltpu.make_async_copy(out.at[:, cols], result.at[:, cols], out_sem.at[chunk])
 
     def finish(chunk, carry):
         for side in range(2):
             second_copy(side, chunk).wait_recv()
         total = own[chunk] + rb2[chunk].astype(F32) + rb2[8 + chunk].astype(F32)
         out[:, pl.ds(pl.multiple_of(chunk * 512, 512), 512)] = total.astype(BF16)
+        store(chunk).start()
         return carry
 
     lax.fori_loop(0, 8, finish, 0)
@@ -460,7 +506,7 @@
     for d in range(1, row_chips):
         for copy in peer_copies(d):
             copy.wait_send()
-    for copy in near_copies + [tail_copy] + list(line_sibling):
+    for copy in near_copies + [pass2] + tail_copies + list(line_sibling):
         copy.wait_send()
 
     @pl.when(x_low == 0)
@@ -482,8 +528,9 @@
             first_copy(side, j).wait_send()
             second_copy(side, j).wait_send()
             second_copy(side, 4 + j).wait_send()
-    for i in range(4):
-        give(i).wait_send()
+    for chunk in range(8):
+        store(chunk).wait()
+    give(y).wait_send()
 
 
 def layer(n, q, k, v, w):
@@ -493,7 +540,7 @@
         functools.partial(kernel, n),
         out_shape=jax.ShapeDtypeStruct((128, 4096), BF16),
         in_specs=[hbm_spec] * 4,
-        out_specs=pl.BlockSpec(memory_space=pltpu.VMEM),
+        out_specs=pl.BlockSpec(memory_space=pl.ANY),
         scratch_shapes=[
             vm((1280, 1024), BF16),
             vm((1024, 512), BF16),
@@ -521,11 +568,12 @@
             vm((16, 128, 512), BF16),
             vm((16, 128, 512), BF16),
             vm((8, 128, 512), F32),
+            vm((128, 4096), BF16),
             pltpu.SemaphoreType.DMA((4,)),
         ]
-        + [pltpu.SemaphoreType.DMA((count,)) for count in (5, 5, 16, 16, 6, 6, 4, 4, 16, 16, 8, 8, 16, 16)],
+        + [pltpu.SemaphoreType.DMA((count,)) for count in (6, 6, 16, 16, 6, 6, 4, 4, 16, 16, 8, 8, 16, 16, 8)],
         compiler_params=pltpu.CompilerParams(
-            collective_id=0, has_side_effects=True, vmem_limit_bytes=56 * 1024 * 1024
+            collective_id=0, has_side_effects=True, vmem_limit_bytes=52 * 1024 * 1024
         ),
         cost_estimate=pl.CostEstimate(flops=6 * 10**9, bytes_accessed=8 * 2**20, transcendentals=2 * 10**6),
     )(q, k, v, w)

time: 90 us -> 80.8 us (0.90)
  the two profiles are of different devices: /device:TPU:34 before, /device:TPU:2 now
where the time goes in v4:
time: 80.8 us
  Pallas kernels  79.8 us (99%)
  local copies, waits for them, and re-layouts  0.97 us (1%)
    pallas_call x1, Pallas kernels, layer(): pl.pallas_call(functools.partial(kernel, n), out_shape=jax.ShapeDtypeStru...  79.8 us

profile of v4, /device:TPU:2, one launch (start us, length us, event | category | flops | bytes accessed | tf_op | source)
XLA Modules:
  0.0 80.8 jit_solution(2689977895064554648)
XLA Ops:
  0.0 79.8 %shard_map.46 = bf16[128,4096]{1,0:T(8,128)(2,1)S(1)} custom-call(bf16[1024,512]{1,0:T(8,128)(2,1)} %q_hbm.1, bf16[1024,512]{1,0:T(8,128)(2,1)} %k_hbm.1, bf16[1024,512]{1,0:T(8,128)(2,1)} %v_hbm.1, bf16[512,4096]{1,0:T(8,128)(2,1)} %w_hbm.1), custom_call_target="tpu_custom_call" | custom-call | flops 6000000000 | bytes 8388608 | tf_op jit(solution)/shard_map/pallas_call | solution.py:539
  79.8 1.0 %copy.6 = bf16[128,4096]{1,0:T(8,128)(2,1)} copy(bf16[128,4096]{1,0:T(8,128)(2,1)S(1)} %shard_map.46) | data formatting | bytes 2097152

commit v5 on v4

--- a/solution.py
+++ b/solution.py
@@ -153,8 +153,6 @@
         return remote(src.at[rows, cols], w_in.at[rows, cols], w_send, w_recv, kind * 4 + j, place)
 
     def place_of(j):
-        if j < 2:
-            return side_x, lax.rem(side_x + 2, 4), x_next
         return side_z, side_z, beside_z
 
     def w_across(j):
@@ -282,9 +280,7 @@
         return carry
 
     w_across(1).start()
-    lax.fori_loop(2, 5, near_step, 0)
-    pass_on(0)
-    lax.fori_loop(5, 6, near_step, 0)
+    lax.fori_loop(2, 6, near_step, 0)
     for d in range(1, row_chips):
         for copy in peer_copies(d):
             copy.wait_recv()
@@ -303,7 +299,6 @@
     for copy in tail_copies:
         copy.wait_recv()
     lax.fori_loop(0, 2, near_step, 0)
-    pass_on(1)
     w_across(3).start()
 
     @pl.when(x_low == 1)
@@ -313,7 +308,12 @@
         for copy in line_last:
             copy.start()
 
-    pass_last(0)
+    @pl.when(x_low == 0)
+    def _():
+        for copy in line_next:
+            copy.wait_send()
+
+    pass_on(0)
     for copy in line_sibling:
         copy.wait_recv()
     for copy in near_copies[1:] + [pass2]:
@@ -323,6 +323,8 @@
     def _():
         for copy in line_last:
             copy.wait_recv()
+
+    pass_on(1)
 
     windows3 = [pl.ds(pl.multiple_of(c * STRIDE3 + chip * 32, 32), 192) for c in range(2)]
     windows4 = [pl.ds(c * 256, 192) for c in range(2)]
@@ -361,8 +363,6 @@
 
     for h in range(4):
         far(h)
-    pass_on(2)
-    pass_last(1)
 
     y_up, y_down, y_far = lax.rem(y + 1, 4), lax.rem(y + 3, 4), lax.rem(y + 2, 4)
 
@@ -398,6 +398,7 @@
     mix_own(y_far)
     mix_out(y_up)
     give(y_up).start()
+    pass_last(0)
     mix_out(y_down)
     mix_own(y_up)
     mix_own(y_down)
@@ -442,10 +443,13 @@
         direct(1, j)
         return carry
 
-    def both(j, carry):
-        begin(j, carry)
-        direct(0, j)
-        direct(1, j)
+    def follow(j, carry):
+        for side in range(2):
+            chunk = 2 * j + side
+            mine = share((y_up, y_down)[side], chunk)
+            first_copy(side, j).wait_recv()
+            sb2[side * 8 + chunk] = (mine + rb1[side * 4 + j].astype(F32)).astype(BF16)
+            second_copy(side, chunk).start()
         return carry
 
     give(y_far).wait_send()
@@ -453,7 +457,8 @@
     give(y_far).wait_recv()
     w_ready(0)
     lax.fori_loop(0, 1, begin, 0)
-    pass_on(3)
+    pass_on(2)
+    pass_last(1)
     w_ready(1)
     lax.fori_loop(1, 2, begin, 0)
     give(y_up).wait_send()
@@ -463,23 +468,17 @@
     give(y_down).wait_send()
     give(y_down).wait_recv()
     lax.fori_loop(0, 2, direct_down, 0)
+    pass_on(3)
+    lax.fori_loop(0, 2, follow, 0)
     pass_last(2)
     w_ready(2)
-    lax.fori_loop(2, 3, both, 0)
+    lax.fori_loop(2, 3, begin, 0)
     pass_last(3)
     w_ready(3)
-    lax.fori_loop(3, 4, both, 0)
-
-    def follow(j, carry):
-        for side in range(2):
-            chunk = 2 * j + side
-            mine = share((y_up, y_down)[side], chunk)
-            first_copy(side, j).wait_recv()
-            sb2[side * 8 + chunk] = (mine + rb1[side * 4 + j].astype(F32)).astype(BF16)
-            second_copy(side, chunk).start()
-        return carry
-
-    lax.fori_loop(0, 4, follow, 0)
+    lax.fori_loop(3, 4, begin, 0)
+    lax.fori_loop(2, 4, direct_up, 0)
+    lax.fori_loop(2, 4, direct_down, 0)
+    lax.fori_loop(2, 4, follow, 0)
 
     give(y).wait_recv()
 
@@ -508,11 +507,6 @@
             copy.wait_send()
     for copy in near_copies + [pass2] + tail_copies + list(line_sibling):
         copy.wait_send()
-
-    @pl.when(x_low == 0)
-    def _():
-        for copy in line_next:
-            copy.wait_send()
 
     @pl.when(x_low == 1)
     def _():

time: 80.8 us -> 75.2 us (0.931)
  the two profiles are of different devices: /device:TPU:2 before, /device:TPU:34 now
where the time goes in v5:
time: 75.2 us; the launch traced here: 74 us
  Pallas kernels  73 us (97%)
  local copies, waits for them, and re-layouts  0.97 us (1%)
    pallas_call x1, Pallas kernels, layer(): pl.pallas_call(functools.partial(kernel, n), out_shape=jax.ShapeDtypeStru...  73 us

profile of v5, /device:TPU:34, one launch (start us, length us, event | category | flops | bytes accessed | tf_op | source)
XLA Modules:
  0.0 74.0 jit_solution(9316233836257547355)
XLA Ops:
  0.0 73.0 %shard_map.46 = bf16[128,4096]{1,0:T(8,128)(2,1)S(1)} custom-call(bf16[1024,512]{1,0:T(8,128)(2,1)} %q_hbm.1, bf16[1024,512]{1,0:T(8,128)(2,1)} %k_hbm.1, bf16[1024,512]{1,0:T(8,128)(2,1)} %v_hbm.1, bf16[512,4096]{1,0:T(8,128)(2,1)} %w_hbm.1), custom_call_target="tpu_custom_call" | custom-call | flops 6000000000 | bytes 8388608 | tf_op jit(solution)/shard_map/pallas_call | solution.py:533
  73.1 1.0 %copy.6 = bf16[128,4096]{1,0:T(8,128)(2,1)} copy(bf16[128,4096]{1,0:T(8,128)(2,1)S(1)} %shard_map.46) | data formatting | bytes 2097152

commit v6 on v5

--- a/solution.py
+++ b/solution.py
@@ -307,11 +307,6 @@
             copy.wait_recv()
         for copy in line_last:
             copy.start()
-
-    @pl.when(x_low == 0)
-    def _():
-        for copy in line_next:
-            copy.wait_send()
 
     pass_on(0)
     for copy in line_sibling:
@@ -398,12 +393,12 @@
     mix_own(y_far)
     mix_out(y_up)
     give(y_up).start()
-    pass_last(0)
     mix_out(y_down)
     mix_own(y_up)
     mix_own(y_down)
     mix_out(y)
     mix_own(y)
+    pass_last(0)
     load_w.wait()
 
     def share(target, chunk):
@@ -457,10 +452,10 @@
     give(y_far).wait_recv()
     w_ready(0)
     lax.fori_loop(0, 1, begin, 0)
-    pass_on(2)
     pass_last(1)
     w_ready(1)
     lax.fori_loop(1, 2, begin, 0)
+    pass_on(2)
     give(y_up).wait_send()
     give(y).start()
     give(y_up).wait_recv()
@@ -507,6 +502,11 @@
             copy.wait_send()
     for copy in near_copies + [pass2] + tail_copies + list(line_sibling):
         copy.wait_send()
+
+    @pl.when(x_low == 0)
+    def _():
+        for copy in line_next:
+            copy.wait_send()
 
     @pl.when(x_low == 1)
     def _():

time: 75.2 us -> 75.2 us (level)
  no operation moved by 1% of the time
where the time goes in v6:
time: 75.2 us; the launch traced here: 74 us
  Pallas kernels  73 us (97%)
  local copies, waits for them, and re-layouts  0.97 us (1%)
    pallas_call x1, Pallas kernels, layer(): pl.pallas_call(functools.partial(kernel, n), out_shape=jax.ShapeDtypeStru...  73 us

profile of v6, /device:TPU:34, one launch (start us, length us, event | category | flops | bytes accessed | tf_op | source)
XLA Modules:
  0.0 74.0 jit_solution(13773059232162485223)
XLA Ops:
  0.0 73.0 %shard_map.46 = bf16[128,4096]{1,0:T(8,128)(2,1)S(1)} custom-call(bf16[1024,512]{1,0:T(8,128)(2,1)} %q_hbm.1, bf16[1024,512]{1,0:T(8,128)(2,1)} %k_hbm.1, bf16[1024,512]{1,0:T(8,128)(2,1)} %v_hbm.1, bf16[512,4096]{1,0:T(8,128)(2,1)} %w_hbm.1), custom_call_target="tpu_custom_call" | custom-call | flops 6000000000 | bytes 8388608 | tf_op jit(solution)/shard_map/pallas_call | solution.py:533
  73.1 1.0 %copy.6 = bf16[128,4096]{1,0:T(8,128)(2,1)} copy(bf16[128,4096]{1,0:T(8,128)(2,1)S(1)} %shard_map.46) | data formatting | bytes 2097152
